TPU v7x, 32 devices: a whole 2x2x4 slice. The times are simulated.
32 devices in a mesh: gx: 4 (over y, x), gy: 4 (over z), gz: 2 (over core).
Axes of the slice: x: 2, y: 2, z: 4, core: 2. Of those that a mesh axis runs over, the one named last changes fastest.
Arguments:
- theta_field: float32 [4, 4, 128, 12288], P('gx', 'gy', 'gz'), may hold values from -6 to 6
- courants: bfloat16 [3, 4, 4, 128, 12288], P(None, 'gx', 'gy', 'gz'), may hold values from -0.27929688 to 0.27929688
- meso_columns: float32 [60, 32768], P(None, ('gx', 'gy', 'gz')), may hold values from -6 to 6
- col_weight: float32 [32768], P(('gx', 'gy', 'gz')), may hold values from 0.25 to 1
- owner_ids: int32 [32768, 1], P(('gx', 'gy', 'gz')), may hold values from 0 to 7; in each aligned block of 1024 rows (0 to 1023, 1024 to 2047, ...) at most 384 rows name the same one
- line_ids: int32 [32768], P(('gx', 'gy', 'gz')), may hold values from 0 to 767
- band_start: int32 [32768], P(('gx', 'gy', 'gz')), may hold values from 0 to 11
Outputs:
- theta_next: float32 [4, 4, 128, 12288], P('gx', 'gy', 'gz')
Inputs may be any that keep to these rules, and one draw needn't show every extreme that they name: `owner_ids`: owner o is fringe side o mod 2 of y tile o div 2. Among the rows of one device no owner appears more than 384 times, and some owner appears exactly 384 times.
All inputs are finite; a program needn't handle non-finite values.
Results may differ from a plain program's by a relative error of at most 0.00059.
Values may be sent and summed in bfloat16 or wider, within the bound.
A program may use at most 128 MiB of HBM per device.

v0:
```python
import functools
import math

import jax
import jax.numpy as jnp
from jax import lax
from jax.experimental import pallas as pl
from jax.experimental.pallas import tpu as pltpu
from jax.sharding import PartitionSpec as P

CX = 16
NY = 3072
ZG = 128
KM = 64
FW = 8
NSTEP = 4
LANES = 128
ROWS = 8

MESH = pl.DeviceIdType.MESH
diffusion = 0.02
highest = lax.Precision.HIGHEST
band_span = 3 * (ZG - 1) // 8 + 2


def extended(array, sides, width, wrap):
    for axis, dim in sides:
        devices, length = (lax.axis_size(axis), array.shape[dim])
        up = [(i, (i + 1) % devices) for i in range(devices if wrap else devices - 1)]
        down = [(j, i) for i, j in up]
        last = lax.slice_in_dim(array, length - width, length, axis=dim)
        initial = lax.slice_in_dim(array, 0, width, axis=dim)
        before = lax.ppermute(last, axis, up)
        after = lax.ppermute(initial, axis, down)
        array = jnp.concatenate([before, array, after], axis=dim)
    return array


def band_matrix():
    levels_z = jnp.arange(ZG, dtype=jnp.int32)
    lower_index = 3 * levels_z // 8
    fraction = (3 * levels_z % 8).astype(jnp.float32) / 8.0
    entries = jnp.arange(band_span, dtype=jnp.int32)[None, :]
    return (1.0 - fraction)[:, None] * (entries == lower_index[:, None]) + fraction[:, None] * (
        entries == lower_index[:, None] + 1
    )


def waves_at(places):
    numbers = jnp.arange(KM, dtype=jnp.int32)
    phases = places[:, None] * numbers[None, :] % NY
    angles = phases.astype(jnp.float32) * (2.0 * math.pi / NY)
    return jnp.concatenate([jnp.cos(angles), jnp.sin(angles)], axis=1)


def mode_scale():
    return jnp.where(jnp.arange(2 * KM, dtype=jnp.int32) % KM == 0, 1.0 / NY, 2.0 / NY).astype(
        jnp.float32
    )


def upwind(state_field, courant_one, ahead_cell, behind_cell):
    return -jnp.maximum(courant_one, 0.0) * (state_field - behind_cell) - jnp.minimum(
        courant_one, 0.0
    ) * (ahead_cell - state_field)


def sweep_once(state_field, courant_local):
    side_cells = extended(state_field, (("gx", 1), ("gy", 2)), 1, True)
    level_cells = extended(state_field, (("gz", 0),), 1, False)
    pairs = (
        (side_cells[:, 2:, 1:-1], side_cells[:, :-2, 1:-1]),
        (level_cells[2:], level_cells[:-2]),
        (side_cells[:, 1:-1, 2:], side_cells[:, 1:-1, :-2]),
    )
    change = 0.0
    neighbours = 0.0
    for direction, (ahead, behind) in enumerate(pairs):
        change = change + upwind(
            state_field, courant_local[direction].astype(jnp.float32), ahead, behind
        )
        neighbours = neighbours + ahead + behind
    return state_field + change + diffusion * (neighbours - 6.0 * state_field)


def target_spectrum(meso_columns, col_weight, owner_ids, line_ids, band_start, tile_rows):
    owners = owner_ids[:, 0]
    places = owners // 2 * tile_rows + line_ids
    waves = waves_at(places) * col_weight[:, None]
    sided = jnp.concatenate(
        [jnp.where((owners % 2 == side)[:, None], waves, 0.0) for side in range(2)], axis=1
    )
    shifted = jnp.zeros((band_span, meso_columns.shape[1]), jnp.float32)
    for offset in range(meso_columns.shape[0] - band_span + 1):
        shifted = shifted + jnp.where(
            band_start[None, :] == offset, meso_columns[offset : offset + band_span], 0.0
        )
    return jnp.dot(shifted, sided, precision=highest, preferred_element_type=jnp.float32)


def sweep_kernel(
    sizes,
    theta_ref,
    courant_ref,
    coef_ref,
    waves_ref,
    out_ref,
    state,
    weight,
    courant,
    coef,
    waves,
    x_send,
    x_recv,
    y_send,
    y_recv,
    in_sem,
    out_sem,
    xs_sem,
    xr_sem,
    ys_sem,
    yr_sem,
    zs_sem,
    zr_sem,
):
    n_gx, n_gy, levels, tiles = sizes
    chunks = levels // ROWS
    planes = CX * tiles
    gx, gy, gz = (lax.axis_index(axis) for axis in ("gx", "gy", "gz"))
    x_right, x_left = lax.rem(gx + 1, n_gx), lax.rem(gx + n_gx - 1, n_gx)
    y_right, y_left = lax.rem(gy + 1, n_gy), lax.rem(gy + n_gy - 1, n_gy)
    other = 1 - gz
    east_end = gx == n_gx - 1
    west_end = gx == 0
    body_rows = pl.ds(ROWS, levels)

    def tile_lanes(tile):
        return pl.ds(pl.multiple_of(tile * LANES, LANES), LANES)

    courant_copy = pltpu.make_async_copy(courant_ref, courant, in_sem.at[1])
    coef_copy = pltpu.make_async_copy(coef_ref, coef, in_sem.at[2])
    waves_copy = pltpu.make_async_copy(waves_ref, waves, in_sem.at[3])

    def fetch(tile, carry):
        pltpu.make_async_copy(
            theta_ref.at[:, tile_lanes(tile)],
            state.at[0, tile + tiles, body_rows, :],
            in_sem.at[0],
        ).start()
        return carry

    courant_copy.start()
    lax.fori_loop(0, planes, fetch, 0)
    coef_copy.start()
    waves_copy.start()

    barrier = pltpu.get_barrier_semaphore()
    neighbours = (
        {"gx": x_right},
        {"gx": x_left},
        {"gy": y_right},
        {"gy": y_left},
        {"gz": other},
    )
    for neighbour in neighbours:
        pl.semaphore_signal(barrier, inc=1, device_id=neighbour, device_id_type=MESH)

    zero_rows = pl.ds(pl.multiple_of(jnp.where(gz == 0, 0, ROWS + levels), ROWS), ROWS)

    def blank(tile, carry):
        for buffer in range(2):
            state[buffer, tile + tiles, zero_rows, :] = jnp.zeros((ROWS, LANES), jnp.float32)
        return carry

    lax.fori_loop(0, planes, blank, 0)
    y_send[...] = jnp.zeros_like(y_send)
    lane = lax.broadcasted_iota(jnp.int32, (ROWS, LANES), 1)

    courant_copy.wait()

    def weigh(tile, carry):
        centre = 1.0
        for direction in range(3):
            number = courant[direction, :, tile_lanes(tile)].astype(jnp.float32)
            upward = jnp.maximum(number, 0.0)
            behind = upward + diffusion
            ahead = (upward - number) + diffusion
            weight[2 * direction + 1, tile] = behind
            weight[2 * direction + 2, tile] = ahead
            centre = centre - (behind + ahead)
        weight[0, tile] = centre
        return carry

    lax.fori_loop(0, planes, weigh, 0)

    whole = state.at[0, pl.ds(tiles, planes), body_rows, :]
    pltpu.make_async_copy(whole, whole, in_sem.at[0]).wait()
    coef_copy.wait()
    waves_copy.wait()

    @pl.when(jnp.logical_or(west_end, east_end))
    def _():
        first = jnp.where(east_end, CX - FW, 0)

        def nudge(index, carry):
            smooth = jnp.dot(
                coef[index], waves[...], precision=highest, preferred_element_type=jnp.float32
            )
            base = (first + index + 1) * tiles
            for tile in range(tiles):
                state[0, base + tile, body_rows, :] += smooth[:, tile * LANES : (tile + 1) * LANES]
            return carry

        lax.fori_loop(0, FW, nudge, 0)

    source_rows = pl.ds(pl.multiple_of(jnp.where(gz == 0, levels, ROWS), ROWS), ROWS)
    target_rows = pl.ds(pl.multiple_of(jnp.where(gz == 0, 0, ROWS + levels), ROWS), ROWS)

    def z_copy(step, group, first, count):
        buffer = lax.rem(step, 2)
        some = pl.ds((first + 1) * tiles, count * tiles)
        return pltpu.make_async_remote_copy(
            src_ref=state.at[buffer, some, source_rows, :],
            dst_ref=state.at[buffer, some, target_rows, :],
            send_sem=zs_sem.at[step, group],
            recv_sem=zr_sem.at[step, group],
            device_id={"gz": other},
            device_id_type=MESH,
        )

    def y_copy(step, group, side):
        return pltpu.make_async_remote_copy(
            src_ref=y_send.at[step, group, side],
            dst_ref=y_recv.at[step, group, side],
            send_sem=ys_sem.at[step, group, side],
            recv_sem=yr_sem.at[step, group, side],
            device_id={"gy": y_right if side == 0 else y_left},
            device_id_type=MESH,
        )

    def x_copy(step, side):
        return pltpu.make_async_remote_copy(
            src_ref=x_send.at[step, side],
            dst_ref=x_recv.at[step, side],
            send_sem=xs_sem.at[step, side],
            recv_sem=xr_sem.at[step, side],
            device_id={"gx": x_right if side == 0 else x_left},
            device_id_type=MESH,
        )

    half = (CX - 2) // 2
    groups = ((1, half), (1 + half, half), (0, 1), (CX - 1, 1))

    def pack(step, group, plane, chunk, low, high):
        place = plane + chunk * CX
        here = lane == place
        y_send[step, group, 0] = jnp.where(
            here, pltpu.roll(high, lax.rem(place + 1, LANES), 1), y_send[step, group, 0]
        )
        y_send[step, group, 1] = jnp.where(
            here, pltpu.roll(low, place, 1), y_send[step, group, 1]
        )

    def send(step, group):
        z_copy(step, group, *groups[group]).start()
        for side in range(2):
            y_copy(step, group, side).start()
        if group >= 2:
            side = 3 - group
            buffer = lax.rem(step, 2)
            base = (groups[group][0] + 1) * tiles
            for tile in range(tiles):
                x_send[step, side, tile] = state[buffer, base + tile, body_rows, :].astype(
                    jnp.bfloat16
                )
            x_copy(step, side).start()

    pl.semaphore_wait(barrier, len(neighbours))

    def plane_of(turn):
        plane = jnp.where(turn < 2 * half, turn + 1, jnp.where(turn == 2 * half, 0, CX - 1))
        group = jnp.where(
            turn < half, 0, jnp.where(turn < 2 * half, 1, jnp.where(turn == 2 * half, 2, 3))
        )
        return plane, group

    def pack_start(turn, carry):
        plane, group = plane_of(turn)
        base = (plane + 1) * tiles
        for chunk in range(chunks):
            rows = pl.ds(ROWS + chunk * ROWS, ROWS)
            pack(
                0, group, plane, chunk, state[0, base, rows, :], state[0, base + tiles - 1, rows, :]
            )
        return carry

    lax.fori_loop(0, CX, pack_start, 0)
    for group in (2, 3, 0, 1):
        send(jnp.int32(0), group)

    starts = (0, half, 2 * half, 2 * half + 1)

    def advance(step, carry):
        now = lax.rem(step, 2)
        later = 1 - now

        def one(turn, carry):
            plane, group = plane_of(turn)
            for which in range(4):

                @pl.when(turn == starts[which])
                def _():
                    z_copy(step, which, *groups[which]).wait_recv()
                    for side in range(2):
                        y_copy(step, which, side).wait_recv()

                    @pl.when(step > 0)
                    def _():
                        z_copy(step - 1, which, *groups[which]).wait_send()

                    if which >= 2:
                        side = which - 2
                        x_copy(step, side).wait_recv()
                        base = 0 if side == 0 else (CX + 1) * tiles
                        for tile in range(tiles):
                            state[now, base + tile, body_rows, :] = x_recv[
                                step, side, tile
                            ].astype(jnp.float32)

            base = (plane + 1) * tiles
            from_left = y_recv[step, group, 0]
            from_right = y_recv[step, group, 1]
            for chunk in range(chunks):
                row = ROWS + chunk * ROWS
                rows = pl.ds(row, ROWS)
                own = pl.ds(chunk * ROWS, ROWS)
                place = plane + chunk * CX
                cells = [state[now, base + tile, rows, :] for tile in range(tiles)]
                up = [pltpu.roll(from_left, lax.rem(LANES - place, LANES), 1)]
                up = up + [pltpu.roll(cell, 1, 1) for cell in cells]
                down = [pltpu.roll(cell, LANES - 1, 1) for cell in cells]
                down = down + [pltpu.roll(from_right, LANES - 1 - place, 1)]
                results = []
                for tile in range(tiles):
                    at = base + tile
                    mine = plane * tiles + tile
                    near = (
                        cells[tile],
                        state[now, at - tiles, rows, :],
                        state[now, at + tiles, rows, :],
                        state[now, at, pl.ds(row - 1, ROWS), :],
                        state[now, at, pl.ds(row + 1, ROWS), :],
                        jnp.where(lane == 0, up[tile], up[tile + 1]),
                        jnp.where(lane == LANES - 1, down[tile + 1], down[tile]),
                    )
                    terms = [weight[k, mine, own, :] * near[k] for k in range(7)]
                    total = ((terms[1] + terms[2]) + (terms[3] + terms[4])) + (
                        (terms[5] + terms[6]) + terms[0]
                    )
                    state[later, at, rows, :] = total
                    results.append(total)

                @pl.when(step < NSTEP - 1)
                def _():
                    pack(step + 1, group, plane, chunk, results[0], results[-1])

            for which in range(4):
                end = starts[which + 1] if which < 3 else CX

                @pl.when(jnp.logical_and(turn == end - 1, step < NSTEP - 1))
                def _():
                    send(step + 1, which)

            @pl.when(step == NSTEP - 1)
            def _():
                for tile in range(tiles):
                    pltpu.make_async_copy(
                        state.at[later, base + tile, body_rows, :],
                        out_ref.at[:, tile_lanes(plane * tiles + tile)],
                        out_sem,
                    ).start()

            return carry

        return lax.fori_loop(0, CX, one, carry)

    lax.fori_loop(0, NSTEP, advance, 0)

    for group in range(4):
        z_copy(NSTEP - 1, group, *groups[group]).wait_send()

    def settle(step, carry):
        for side in range(2):
            x_copy(step, side).wait_send()
            for group in range(4):
                y_copy(step, group, side).wait_send()
        return carry

    lax.fori_loop(0, NSTEP, settle, 0)
    pltpu.make_async_copy(whole, whole, out_sem).wait()


def fast_sweep(theta, courants, coef, waves, n_gx, n_gy, tile_rows):
    levels = theta.shape[0]
    tiles = tile_rows // LANES
    planes = CX * tiles
    slots = (CX + 2) * tiles
    dma = pltpu.SemaphoreType.DMA
    anywhere = pl.BlockSpec(memory_space=pl.ANY)
    return pl.pallas_call(
        functools.partial(sweep_kernel, (n_gx, n_gy, levels, tiles)),
        out_shape=jax.ShapeDtypeStruct(theta.shape, jnp.float32),
        in_specs=[anywhere] * 4,
        out_specs=anywhere,
        scratch_shapes=[
            pltpu.VMEM((2, slots, levels + 2 * ROWS, LANES), jnp.float32),
            pltpu.VMEM((7, planes, levels, LANES), jnp.float32),
            pltpu.VMEM(courants.shape, jnp.bfloat16),
            pltpu.VMEM(coef.shape, jnp.float32),
            pltpu.VMEM(waves.shape, jnp.float32),
            pltpu.VMEM((NSTEP, 2, tiles, levels, LANES), jnp.bfloat16),
            pltpu.VMEM((NSTEP, 2, tiles, levels, LANES), jnp.bfloat16),
            pltpu.VMEM((NSTEP, 4, 2, ROWS, LANES), jnp.float32),
            pltpu.VMEM((NSTEP, 4, 2, ROWS, LANES), jnp.float32),
            dma((4,)),
            dma,
            dma((NSTEP, 2)),
            dma((NSTEP, 2)),
            dma((NSTEP, 4, 2)),
            dma((NSTEP, 4, 2)),
            dma((NSTEP, 4)),
            dma((NSTEP, 4)),
        ],
        compiler_params=pltpu.CompilerParams(
            collective_id=0, has_side_effects=True, vmem_limit_bytes=58 * 1024 * 1024
        ),
        name="transport",
    )(theta, courants, coef, waves)


def body(theta_field, courants, meso_columns, col_weight, owner_ids, line_ids, band_start):
    n_gx, n_gy, n_gz = (lax.axis_size(axis) for axis in ("gx", "gy", "gz"))
    tile_rows = NY // n_gy
    levels = theta_field.shape[2]
    theta_local = theta_field.reshape(levels, CX * tile_rows)
    courant_local = courants.reshape(3, levels, CX * tile_rows)
    column_index = lax.axis_index("gx")
    east_end = column_index == n_gx - 1
    west_end = column_index == 0

    sums = target_spectrum(meso_columns, col_weight, owner_ids, line_ids, band_start, tile_rows)
    sums = lax.psum(sums, ("gx", "gy", "gz"))
    side_sums = jnp.where(east_end, sums[:, 2 * KM :], sums[:, : 2 * KM])
    bands = lax.dynamic_slice_in_dim(band_matrix(), lax.axis_index("gz") * levels, levels, axis=0)
    target = jnp.dot(bands, side_sums, precision=highest, preferred_element_type=jnp.float32)

    own_waves = waves_at(lax.axis_index("gy") * tile_rows + jnp.arange(tile_rows, dtype=jnp.int32))
    width = FW * tile_rows
    strip = jnp.where(east_end, theta_local[:, -width:], theta_local[:, :width])
    strip = strip.reshape(levels, FW, tile_rows).transpose(1, 0, 2)
    spectrum = jnp.einsum(
        "xky,ym->xkm", strip, own_waves, precision=highest, preferred_element_type=jnp.float32
    )
    spectrum = target[None] - lax.psum(spectrum, "gy")
    offsets = jnp.arange(FW, dtype=jnp.float32)
    relaxation = jnp.where(
        east_end, (offsets + 1.0) / FW, jnp.where(west_end, (FW - offsets) / FW, 0.0)
    )
    coef = spectrum * mode_scale()[None, None, :] * relaxation[:, None, None]

    if tile_rows % LANES == 0 and levels == 64 and n_gz == 2 and n_gx > 2 and n_gy > 2:
        result = fast_sweep(
            theta_local, courant_local, coef, own_waves.T, n_gx, n_gy, tile_rows
        )
        return result.reshape(1, 1, levels, CX * tile_rows)

    update = jnp.einsum(
        "xkm,ym->kxy", coef, own_waves, precision=highest, preferred_element_type=jnp.float32
    )
    state_field = theta_local.reshape(levels, CX, tile_rows)
    state_field = jnp.where(
        east_end,
        state_field.at[:, CX - FW :].add(update),
        state_field.at[:, :FW].add(update),
    )
    courant_field = courant_local.reshape(3, levels, CX, tile_rows)
    for step_index in range(NSTEP):
        state_field = sweep_once(state_field, courant_field)
    return state_field.reshape(1, 1, levels, CX * tile_rows)


def solution(mesh):
    in_specs = (
        P("gx", "gy", "gz", None),
        P(None, "gx", "gy", "gz", None),
        P(None, ("gx", "gy", "gz")),
        P(("gx", "gy", "gz")),
        P(("gx", "gy", "gz"), None),
        P(("gx", "gy", "gz")),
        P(("gx", "gy", "gz")),
    )
    out_specs = P("gx", "gy", "gz", None)
    return jax.shard_map(body, mesh=mesh, in_specs=in_specs, out_specs=out_specs, check_vma=False)
```

profile of v0, /device:TPU:0, one launch (start us, length us, event | category | flops | bytes accessed | tf_op | source)
XLA Modules:
  0.0 178.2 jit_solution(17435888265615003164)
XLA Ops:
  6.5 0.0 all-reduce.2.cloned.1.call-start
  6.5 0.8 fusion.55
  7.4 2.0 %slice_select_fusion = f32[64,6144]{1,0:T(8,128)S(1)} fusion(f32[64,12288]{1,0:T(8,128)} %bitcast.16, pred[]{:T(512)S(6)} %eq.147), kind=kLoop, calls=%fused_computation.3 | loop fusion | flops 393216 | bytes 4718593 | tf_op jit(solution)/shard_map/jit(_where)/select_n | solution.py:459
  9.4 0.0 copy-start
  9.4 0.0 copy-start.3
  9.4 0.0 copy-start.2
  9.4 2.1 %fusion = f32[8,64,128]{2,1,0:T(8,128)} fusion(f32[8,8,8,768]{3,2,1,0:T(8,128)S(1)} %bitcast.19, f32[768,64]{0,1:T(8,128)S(1)} %get-tuple-element.24, f32[768,64]{0,1:T(8,128)S(1)} %get-tuple-element.23), kind=kOutput, calls=%fused_computation.1 | convolution fusion | flops 604078080 | bytes 2228224 | tf_op jit(solution)/shard_map/xky,ym->xkm/dot_general | solution.py:461
  11.5 0.0 copy-start.1
  11.5 0.0 all-reduce.2.cloned.1.call-update
  11.6 0.8 fusion.14.waves_ref
  12.4 0.0 copy-done
  12.5 0.0 copy-done.3
  12.5 0.0 copy-done.2
  12.5 0.0 copy-start.4
  12.5 2.2 %fusion.11 = (f32[1024,64]{1,0:T(8,128)S(1)}, f32[1024,64]{1,0:T(8,128)S(1)}) fusion(s32[1024]{0:T(1024)S(1)} %fusion.83), kind=kLoop, calls=%fused_computation.16 | loop fusion | flops 589824 | bytes 528384 | tf_op jit(solution)/shard_map/cos | solution.py:53
  14.7 0.0 copy-done.1
  14.7 0.9 broadcast_select_fusion.1
  15.6 0.0 copy-done.4
  15.6 1.0 fusion.2
  16.7 0.1 dynamic-slice.1
  16.8 0.1 dynamic-slice.2
  16.9 0.1 dynamic-slice.3
  16.9 0.1 dynamic-slice
  17.0 42.6 %psum.14 = f32[49,256]{1,0:T(8,128)S(1)} all-reduce(f32[49,256]{1,0:T(8,128)S(1)} %fusion.2), channel_id=1, replica_groups=mesh['gx'=4,'gy'=4,'gz'=2] {'gx','gy','gz'}, use_global_device_ids=true, to_apply=%region_0.1 | all-reduce | flops 12544 | bytes 100352 | tf_op jit(solution)/shard_map/psum | solution.py:452
  59.7 0.2 fusion.70
  59.9 0.0 all-reduce.2.cloned.1.call-done
  59.9 1.7 multiply_multiply_fusion.coef_ref
  61.7 105.9 %transport.1 = f32[64,12288]{1,0:T(8,128)} custom-call(f32[64,12288]{1,0:T(8,128)} %bitcast.17, bf16[3,64,12288]{2,1,0:T(8,128)(2,1)} %bitcast.20, f32[8,64,128]{2,1,0:T(8,128)} %multiply_multiply_fusion.coef_ref, f32[128,768]{1,0:T(8,128)} %fusion.14.waves_ref), custom_call_target="tpu_custom_call" | custom-call | tf_op jit(solution)/shard_map/transport/pallas_call | solution.py:410
  167.6 3.8 %copy.19 = f32[1,1,64,12288]{3,2,1,0:T(8,128)} copy(f32[1,1,64,12288]{3,2,1,0:T(8,128)} %bitcast.18) | data formatting | bytes 6291456
  (10 shorter events, 0.1 us)
Async XLA Ops:
  6.5 53.4 %all-reduce.2.cloned.1.call-start = ((), (), s32[]{:S(2)}) async-start(), calls=%async_computation | async-start | bytes 524288 | tf_op jit(solution)/shard_map/psum | solution.py:464
  9.4 3.0 %copy-start = (s32[1024,1]{0,1:T(1,128)S(1)}, s32[1024,1]{0,1:T(1,128)}, u32[]{:S(2)}) copy-start(s32[1024,1]{0,1:T(1,128)} %param.11) | copy-start | bytes 12292
  9.4 3.0 %copy-start.3 = (s32[1024]{0:T(1024)S(1)}, s32[1024]{0:T(1024)}, u32[]{:S(2)}) copy-start(s32[1024]{0:T(1024)} %param.13) | copy-start | bytes 12292
  9.4 3.1 %copy-start.2 = (s32[1024]{0:T(1024)S(1)}, s32[1024]{0:T(1024)}, u32[]{:S(2)}) copy-start(s32[1024]{0:T(1024)} %param.12) | copy-start | bytes 12292
  11.5 3.2 %copy-start.1 = (f32[1024]{0:T(1024)S(1)}, f32[1024]{0:T(1024)}, u32[]{:S(2)}) copy-start(f32[1024]{0:T(1024)} %param.10) | copy-start | bytes 12292
  12.5 3.1 %copy-start.4 = (f32[60,1024]{1,0:T(8,128)S(1)}, f32[60,1024]{1,0:T(8,128)}, u32[]{:S(2)}) copy-start(f32[60,1024]{1,0:T(8,128)} %param.9) | copy-start | bytes 737284
Sparse Core Ops, SparseCore 0:
  11.7 37.9 all-reduce.1
where the time goes:
time: 179 us; the launch traced here: 178 us
  Pallas kernels  106 us (59%)
  blocking collectives  42.6 us (24%)
  between operations  13.6 us (8%)
  other arithmetic  8.58 us (5%)
  local copies, waits for them, and re-layouts  4.11 us (2%)
  matrix products  3.37 us (2%)
    pallas_call x1, Pallas kernels, fast_sweep(): pl.pallas_call(functools.partial(sweep_kernel, (n_gx, n_gy, levels, tiles...  106 us
    psum x1, blocking collectives, body(): sums = lax.psum(sums, ('gx', 'gy', 'gz'))  42.6 us
    unnamed x11, local copies, waits for them, and re-layouts  3.81 us
  transfers between devices with their start and end apart: 1, of which 0 were waited for; matrix products, arithmetic and copies ran while one was open for 3% of the time, Pallas kernels for 0%

commit v1 on v0

--- a/solution.py
+++ b/solution.py
@@ -105,7 +105,8 @@
     coef_ref,
     waves_ref,
     out_ref,
-    state,
+    state_a,
+    state_b,
     weight,
     courant,
     coef,
@@ -144,7 +145,7 @@
     def fetch(tile, carry):
         pltpu.make_async_copy(
             theta_ref.at[:, tile_lanes(tile)],
-            state.at[0, tile + tiles, body_rows, :],
+            state_a.at[tile + tiles, body_rows, :],
             in_sem.at[0],
         ).start()
         return carry
@@ -168,8 +169,8 @@
     zero_rows = pl.ds(pl.multiple_of(jnp.where(gz == 0, 0, ROWS + levels), ROWS), ROWS)
 
     def blank(tile, carry):
-        for buffer in range(2):
-            state[buffer, tile + tiles, zero_rows, :] = jnp.zeros((ROWS, LANES), jnp.float32)
+        for state in (state_a, state_b):
+            state[tile + tiles, zero_rows, :] = jnp.zeros((ROWS, LANES), jnp.float32)
         return carry
 
     lax.fori_loop(0, planes, blank, 0)
@@ -193,7 +194,7 @@
 
     lax.fori_loop(0, planes, weigh, 0)
 
-    whole = state.at[0, pl.ds(tiles, planes), body_rows, :]
+    whole = state_a.at[pl.ds(tiles, planes), body_rows, :]
     pltpu.make_async_copy(whole, whole, in_sem.at[0]).wait()
     coef_copy.wait()
     waves_copy.wait()
@@ -208,7 +209,7 @@
             )
             base = (first + index + 1) * tiles
             for tile in range(tiles):
-                state[0, base + tile, body_rows, :] += smooth[:, tile * LANES : (tile + 1) * LANES]
+                state_a[base + tile, body_rows, :] += smooth[:, tile * LANES : (tile + 1) * LANES]
             return carry
 
         lax.fori_loop(0, FW, nudge, 0)
@@ -216,12 +217,12 @@
     source_rows = pl.ds(pl.multiple_of(jnp.where(gz == 0, levels, ROWS), ROWS), ROWS)
     target_rows = pl.ds(pl.multiple_of(jnp.where(gz == 0, 0, ROWS + levels), ROWS), ROWS)
 
-    def z_copy(step, group, first, count):
-        buffer = lax.rem(step, 2)
+    def z_copy(state, step, group):
+        first, count = groups[group]
         some = pl.ds((first + 1) * tiles, count * tiles)
         return pltpu.make_async_remote_copy(
-            src_ref=state.at[buffer, some, source_rows, :],
-            dst_ref=state.at[buffer, some, target_rows, :],
+            src_ref=state.at[some, source_rows, :],
+            dst_ref=state.at[some, target_rows, :],
             send_sem=zs_sem.at[step, group],
             recv_sem=zr_sem.at[step, group],
             device_id={"gz": other},
@@ -251,28 +252,25 @@
     half = (CX - 2) // 2
     groups = ((1, half), (1 + half, half), (0, 1), (CX - 1, 1))
 
-    def pack(step, group, plane, chunk, low, high):
-        place = plane + chunk * CX
-        here = lane == place
-        y_send[step, group, 0] = jnp.where(
-            here, pltpu.roll(high, lax.rem(place + 1, LANES), 1), y_send[step, group, 0]
-        )
-        y_send[step, group, 1] = jnp.where(
-            here, pltpu.roll(low, place, 1), y_send[step, group, 1]
-        )
-
-    def send(step, group):
-        z_copy(step, group, *groups[group]).start()
+    def pack(step, group, plane, edges):
+        right, left = y_send[step, group, 0], y_send[step, group, 1]
+        for chunk, (low, high) in enumerate(edges):
+            place = plane + chunk * CX
+            here = lane == place
+            right = jnp.where(here, pltpu.roll(high, lax.rem(place + 1, LANES), 1), right)
+            left = jnp.where(here, pltpu.roll(low, place, 1), left)
+        y_send[step, group, 0] = right
+        y_send[step, group, 1] = left
+
+    def send(state, step, group):
+        z_copy(state, step, group).start()
         for side in range(2):
             y_copy(step, group, side).start()
         if group >= 2:
             side = 3 - group
-            buffer = lax.rem(step, 2)
             base = (groups[group][0] + 1) * tiles
             for tile in range(tiles):
-                x_send[step, side, tile] = state[buffer, base + tile, body_rows, :].astype(
-                    jnp.bfloat16
-                )
+                x_send[step, side, tile] = state[base + tile, body_rows, :].astype(jnp.bfloat16)
             x_copy(step, side).start()
 
     pl.semaphore_wait(barrier, len(neighbours))
@@ -287,55 +285,53 @@
     def pack_start(turn, carry):
         plane, group = plane_of(turn)
         base = (plane + 1) * tiles
+        edges = []
         for chunk in range(chunks):
             rows = pl.ds(ROWS + chunk * ROWS, ROWS)
-            pack(
-                0, group, plane, chunk, state[0, base, rows, :], state[0, base + tiles - 1, rows, :]
-            )
+            edges.append((state_a[base, rows, :], state_a[base + tiles - 1, rows, :]))
+        pack(0, group, plane, edges)
         return carry
 
     lax.fori_loop(0, CX, pack_start, 0)
     for group in (2, 3, 0, 1):
-        send(jnp.int32(0), group)
+        send(state_a, 0, group)
 
     starts = (0, half, 2 * half, 2 * half + 1)
 
-    def advance(step, carry):
-        now = lax.rem(step, 2)
-        later = 1 - now
-
+    def advance(step, now, later, final):
         def one(turn, carry):
             plane, group = plane_of(turn)
             for which in range(4):
 
                 @pl.when(turn == starts[which])
                 def _():
-                    z_copy(step, which, *groups[which]).wait_recv()
+                    z_copy(now, step, which).wait_recv()
                     for side in range(2):
                         y_copy(step, which, side).wait_recv()
 
                     @pl.when(step > 0)
                     def _():
-                        z_copy(step - 1, which, *groups[which]).wait_send()
+                        z_copy(later, step - 1, which).wait_send()
 
                     if which >= 2:
                         side = which - 2
                         x_copy(step, side).wait_recv()
                         base = 0 if side == 0 else (CX + 1) * tiles
                         for tile in range(tiles):
-                            state[now, base + tile, body_rows, :] = x_recv[
-                                step, side, tile
-                            ].astype(jnp.float32)
+                            now[base + tile, body_rows, :] = x_recv[step, side, tile].astype(
+                                jnp.float32
+                            )
 
             base = (plane + 1) * tiles
             from_left = y_recv[step, group, 0]
             from_right = y_recv[step, group, 1]
+            edges = []
             for chunk in range(chunks):
                 row = ROWS + chunk * ROWS
                 rows = pl.ds(row, ROWS)
                 own = pl.ds(chunk * ROWS, ROWS)
                 place = plane + chunk * CX
-                cells = [state[now, base + tile, rows, :] for tile in range(tiles)]
+                cells = [now[base + tile, rows, :] for tile in range(tiles)]
                 up = [pltpu.roll(from_left, lax.rem(LANES - place, LANES), 1)]
                 up = up + [pltpu.roll(cell, 1, 1) for cell in cells]
                 down = [pltpu.roll(cell, LANES - 1, 1) for cell in cells]
@@ -346,10 +342,10 @@
                     mine = plane * tiles + tile
                     near = (
                         cells[tile],
-                        state[now, at - tiles, rows, :],
-                        state[now, at + tiles, rows, :],
-                        state[now, at, pl.ds(row - 1, ROWS), :],
-                        state[now, at, pl.ds(row + 1, ROWS), :],
+                        now[at - tiles, rows, :],
+                        now[at + tiles, rows, :],
+                        now[at, pl.ds(row - 1, ROWS), :],
+                        now[at, pl.ds(row + 1, ROWS), :],
                         jnp.where(lane == 0, up[tile], up[tile + 1]),
                         jnp.where(lane == LANES - 1, down[tile + 1], down[tile]),
                     )
@@ -357,37 +353,42 @@
                     total = ((terms[1] + terms[2]) + (terms[3] + terms[4])) + (
                         (terms[5] + terms[6]) + terms[0]
                     )
-                    state[later, at, rows, :] = total
+                    later[at, rows, :] = total
                     results.append(total)
-
-                @pl.when(step < NSTEP - 1)
-                def _():
-                    pack(step + 1, group, plane, chunk, results[0], results[-1])
+                edges.append((results[0], results[-1]))
+            pack(step + 1, group, plane, edges)
 
             for which in range(4):
                 end = starts[which + 1] if which < 3 else CX
 
                 @pl.when(jnp.logical_and(turn == end - 1, step < NSTEP - 1))
                 def _():
-                    send(step + 1, which)
-
-            @pl.when(step == NSTEP - 1)
-            def _():
-                for tile in range(tiles):
-                    pltpu.make_async_copy(
-                        state.at[later, base + tile, body_rows, :],
-                        out_ref.at[:, tile_lanes(plane * tiles + tile)],
-                        out_sem,
-                    ).start()
+                    send(later, step + 1, which)
+
+            if final:
+
+                @pl.when(step == NSTEP - 1)
+                def _():
+                    for tile in range(tiles):
+                        pltpu.make_async_copy(
+                            later.at[base + tile, body_rows, :],
+                            out_ref.at[:, tile_lanes(plane * tiles + tile)],
+                            out_sem,
+                        ).start()
 
             return carry
 
-        return lax.fori_loop(0, CX, one, carry)
-
-    lax.fori_loop(0, NSTEP, advance, 0)
+        lax.fori_loop(0, CX, one, 0)
+
+    def two(pair, carry):
+        advance(2 * pair, state_a, state_b, False)
+        advance(2 * pair + 1, state_b, state_a, True)
+        return carry
+
+    lax.fori_loop(0, NSTEP // 2, two, 0)
 
     for group in range(4):
-        z_copy(NSTEP - 1, group, *groups[group]).wait_send()
+        z_copy(state_b, NSTEP - 1, group).wait_send()
 
     def settle(step, carry):
         for side in range(2):
@@ -413,14 +414,15 @@
         in_specs=[anywhere] * 4,
         out_specs=anywhere,
         scratch_shapes=[
-            pltpu.VMEM((2, slots, levels + 2 * ROWS, LANES), jnp.float32),
+            pltpu.VMEM((slots, levels + 2 * ROWS, LANES), jnp.float32),
+            pltpu.VMEM((slots, levels + 2 * ROWS, LANES), jnp.float32),
             pltpu.VMEM((7, planes, levels, LANES), jnp.float32),
             pltpu.VMEM(courants.shape, jnp.bfloat16),
             pltpu.VMEM(coef.shape, jnp.float32),
             pltpu.VMEM(waves.shape, jnp.float32),
             pltpu.VMEM((NSTEP, 2, tiles, levels, LANES), jnp.bfloat16),
             pltpu.VMEM((NSTEP, 2, tiles, levels, LANES), jnp.bfloat16),
-            pltpu.VMEM((NSTEP, 4, 2, ROWS, LANES), jnp.float32),
+            pltpu.VMEM((NSTEP + 1, 4, 2, ROWS, LANES), jnp.float32),
             pltpu.VMEM((NSTEP, 4, 2, ROWS, LANES), jnp.float32),
             dma((4,)),
             dma,

time: 179 us -> 110 us (0.61)
  Pallas kernels: 106 us -> 37.4 us
    pallas_call x1, Pallas kernels: 106 us -> 37.4 us  [fast_sweep(): pl.pallas_call(functools.partial(sweep_kernel, (n_gx, n_gy, levels, tiles...]
  transfers between devices with their start and end apart: 1 -> 1, of which waited for: 0 -> 0; matrix products, arithmetic and copies ran while one was open for 3% -> 5% of each run, Pallas kernels for 0% -> 0%
where the time goes in v1:
time: 110 us
  blocking collectives  42.6 us (39%)
  Pallas kernels  37.4 us (34%)
  between operations  13.6 us (12%)
  other arithmetic  8.58 us (8%)
  local copies, waits for them, and re-layouts  4.11 us (4%)
  matrix products  3.37 us (3%)
    psum x1, blocking collectives, body(): sums = lax.psum(sums, ('gx', 'gy', 'gz'))  42.6 us
    pallas_call x1, Pallas kernels, fast_sweep(): pl.pallas_call(functools.partial(sweep_kernel, (n_gx, n_gy, levels, tiles...  37.4 us
    unnamed x11, local copies, waits for them, and re-layouts  3.81 us
    cos x2, other arithmetic, waves_at(): return jnp.concatenate([jnp.cos(angles), jnp.sin(angles)], axis=1)  2.98 us
  transfers between devices with their start and end apart: 1, of which 0 were waited for; matrix products, arithmetic and copies ran while one was open for 5% of the time, Pallas kernels for 0%

profile of v1, /device:TPU:0, one launch (start us, length us, event | category | flops | bytes accessed | tf_op | source)
XLA Modules:
  0.0 109.7 jit_solution(10645995146552355266)
XLA Ops:
  6.5 0.0 all-reduce.2.cloned.1.call-start
  6.5 0.8 fusion.55
  7.4 2.0 %slice_select_fusion = f32[64,6144]{1,0:T(8,128)S(1)} fusion(f32[64,12288]{1,0:T(8,128)} %bitcast.16, pred[]{:T(512)S(6)} %eq.147), kind=kLoop, calls=%fused_computation.3 | loop fusion | flops 393216 | bytes 4718593 | tf_op jit(solution)/shard_map/jit(_where)/select_n | solution.py:461
  9.4 0.0 copy-start
  9.4 0.0 copy-start.3
  9.4 0.0 copy-start.2
  9.4 2.1 %fusion = f32[8,64,128]{2,1,0:T(8,128)} fusion(f32[8,8,8,768]{3,2,1,0:T(8,128)S(1)} %bitcast.19, f32[768,64]{0,1:T(8,128)S(1)} %get-tuple-element.24, f32[768,64]{0,1:T(8,128)S(1)} %get-tuple-element.23), kind=kOutput, calls=%fused_computation.1 | convolution fusion | flops 604078080 | bytes 2228224 | tf_op jit(solution)/shard_map/xky,ym->xkm/dot_general | solution.py:463
  11.5 0.0 copy-start.1
  11.5 0.0 all-reduce.2.cloned.1.call-update
  11.6 0.8 fusion.14.waves_ref
  12.4 0.0 copy-done
  12.5 0.0 copy-done.3
  12.5 0.0 copy-done.2
  12.5 0.0 copy-start.4
  12.5 2.2 %fusion.11 = (f32[1024,64]{1,0:T(8,128)S(1)}, f32[1024,64]{1,0:T(8,128)S(1)}) fusion(s32[1024]{0:T(1024)S(1)} %fusion.83), kind=kLoop, calls=%fused_computation.16 | loop fusion | flops 589824 | bytes 528384 | tf_op jit(solution)/shard_map/cos | solution.py:53
  14.7 0.0 copy-done.1
  14.7 0.9 broadcast_select_fusion.1
  15.6 0.0 copy-done.4
  15.6 1.0 fusion.2
  16.7 0.1 dynamic-slice.1
  16.8 0.1 dynamic-slice.2
  16.9 0.1 dynamic-slice.3
  16.9 0.1 dynamic-slice
  17.0 42.6 %psum.14 = f32[49,256]{1,0:T(8,128)S(1)} all-reduce(f32[49,256]{1,0:T(8,128)S(1)} %fusion.2), channel_id=1, replica_groups=mesh['gx'=4,'gy'=4,'gz'=2] {'gx','gy','gz'}, use_global_device_ids=true, to_apply=%region_0.1 | all-reduce | flops 12544 | bytes 100352 | tf_op jit(solution)/shard_map/psum | solution.py:454
  59.7 0.2 fusion.70
  59.9 0.0 all-reduce.2.cloned.1.call-done
  59.9 1.7 %multiply_multiply_fusion.coef_ref = f32[8,64,128]{2,1,0:T(8,128)} fusion(f32[8,64,128]{2,1,0:T(8,128)} %all-reduce.2.cloned.1.call-done, f32[8]{0:T(128)S(1)} %broadcast_select_fusion.3, f32[128]{0:T(128)S(1)} %compare_select_fusion.2, f32[64,128]{1,0:T(8,128)S(1)} %fusion.70), kind=kLoop, calls=%fused_computation.22 | loop fusion | flops 196608 | bytes 557600 | tf_op jit(solution)/shard_map/mul | solution.py:471
  61.7 37.4 %transport.1 = f32[64,12288]{1,0:T(8,128)} custom-call(f32[64,12288]{1,0:T(8,128)} %bitcast.17, bf16[3,64,12288]{2,1,0:T(8,128)(2,1)} %bitcast.20, f32[8,64,128]{2,1,0:T(8,128)} %multiply_multiply_fusion.coef_ref, f32[128,768]{1,0:T(8,128)} %fusion.14.waves_ref), custom_call_target="tpu_custom_call" | custom-call | tf_op jit(solution)/shard_map/transport/pallas_call | solution.py:411
  99.1 3.8 %copy.19 = f32[1,1,64,12288]{3,2,1,0:T(8,128)} copy(f32[1,1,64,12288]{3,2,1,0:T(8,128)} %bitcast.18) | data formatting | bytes 6291456
  (10 shorter events, 0.1 us)
Async XLA Ops:
  6.5 53.4 %all-reduce.2.cloned.1.call-start = ((), (), s32[]{:S(2)}) async-start(), calls=%async_computation | async-start | bytes 524288 | tf_op jit(solution)/shard_map/psum | solution.py:466
  9.4 3.0 %copy-start = (s32[1024,1]{0,1:T(1,128)S(1)}, s32[1024,1]{0,1:T(1,128)}, u32[]{:S(2)}) copy-start(s32[1024,1]{0,1:T(1,128)} %param.11) | copy-start | bytes 12292
  9.4 3.0 %copy-start.3 = (s32[1024]{0:T(1024)S(1)}, s32[1024]{0:T(1024)}, u32[]{:S(2)}) copy-start(s32[1024]{0:T(1024)} %param.13) | copy-start | bytes 12292
  9.4 3.1 %copy-start.2 = (s32[1024]{0:T(1024)S(1)}, s32[1024]{0:T(1024)}, u32[]{:S(2)}) copy-start(s32[1024]{0:T(1024)} %param.12) | copy-start | bytes 12292
  11.5 3.2 %copy-start.1 = (f32[1024]{0:T(1024)S(1)}, f32[1024]{0:T(1024)}, u32[]{:S(2)}) copy-start(f32[1024]{0:T(1024)} %param.10) | copy-start | bytes 12292
  12.5 3.1 %copy-start.4 = (f32[60,1024]{1,0:T(8,128)S(1)}, f32[60,1024]{1,0:T(8,128)}, u32[]{:S(2)}) copy-start(f32[60,1024]{1,0:T(8,128)} %param.9) | copy-start | bytes 737284
Sparse Core Ops, SparseCore 0:
  11.7 37.9 all-reduce.1

commit v2 on v1

--- a/solution.py
+++ b/solution.py
@@ -21,6 +21,9 @@
 diffusion = 0.02
 highest = lax.Precision.HIGHEST
 band_span = 3 * (ZG - 1) // 8 + 2
+ENTRIES = 64
+BAND_STEP = 24
+BAND_ROWS = 32
 
 
 def extended(array, sides, width, wrap):
@@ -98,19 +101,62 @@
     return jnp.dot(shifted, sided, precision=highest, preferred_element_type=jnp.float32)
 
 
+def waves_of(places):
+    numbers = lax.broadcasted_iota(jnp.int32, (KM, places.shape[1]), 0).astype(jnp.float32)
+    turns = numbers * places
+    quarter = NY // 4
+    quarters = jnp.floor(turns * (1.0 / quarter) + 0.5)
+    angle = (turns - quarter * quarters) * (2.0 * math.pi / NY)
+    square = angle * angle
+    sine = 1.0 / 362880.0
+    for factor in (-1.0 / 5040.0, 1.0 / 120.0, -1.0 / 6.0, 1.0):
+        sine = sine * square + factor
+    sine = sine * angle
+    cosine = 1.0 / 40320.0
+    for factor in (-1.0 / 720.0, 1.0 / 24.0, -0.5, 1.0):
+        cosine = cosine * square + factor
+    corner = quarters - 4.0 * jnp.floor(quarters * 0.25)
+    odd = jnp.logical_or(corner == 1.0, corner == 3.0)
+    cos_values = jnp.where(odd, sine, cosine)
+    sin_values = jnp.where(odd, cosine, sine)
+    cos_values = jnp.where(
+        jnp.logical_or(corner == 1.0, corner == 2.0), -cos_values, cos_values
+    )
+    sin_values = jnp.where(corner >= 2.0, -sin_values, sin_values)
+    return jnp.concatenate([cos_values, sin_values], axis=0)
+
+
+def dot_rows(left, right):
+    return lax.dot_general(
+        left,
+        right,
+        (((1,), (1,)), ((), ())),
+        precision=highest,
+        preferred_element_type=jnp.float32,
+    )
+
+
 def sweep_kernel(
     sizes,
     theta_ref,
     courant_ref,
-    coef_ref,
-    waves_ref,
+    meso_ref,
+    col_weight_ref,
+    codes_ref,
     out_ref,
     state_a,
     state_b,
     weight,
     courant,
+    meso,
+    col_weight,
+    codes,
+    waves,
+    sum_send,
+    sum_recv,
+    part,
+    part_recv,
     coef,
-    waves,
     x_send,
     x_recv,
     y_send,
@@ -123,6 +169,12 @@
     yr_sem,
     zs_sem,
     zr_sem,
+    ss_sem,
+    sr_sem,
+    ps_sem,
+    pr_sem,
+    cs_sem,
+    cr_sem,
 ):
     n_gx, n_gy, levels, tiles = sizes
     chunks = levels // ROWS
@@ -139,8 +191,11 @@
         return pl.ds(pl.multiple_of(tile * LANES, LANES), LANES)
 
     courant_copy = pltpu.make_async_copy(courant_ref, courant, in_sem.at[1])
-    coef_copy = pltpu.make_async_copy(coef_ref, coef, in_sem.at[2])
-    waves_copy = pltpu.make_async_copy(waves_ref, waves, in_sem.at[3])
+    column_copies = [
+        pltpu.make_async_copy(meso_ref, meso, in_sem.at[2]),
+        pltpu.make_async_copy(col_weight_ref, col_weight, in_sem.at[3]),
+        pltpu.make_async_copy(codes_ref, codes, in_sem.at[4]),
+    ]
 
     def fetch(tile, carry):
         pltpu.make_async_copy(
@@ -150,21 +205,77 @@
         ).start()
         return carry
 
+    for copy in column_copies:
+        copy.start()
+    lax.fori_loop(0, planes, fetch, 0)
     courant_copy.start()
-    lax.fori_loop(0, planes, fetch, 0)
-    coef_copy.start()
-    waves_copy.start()
 
     barrier = pltpu.get_barrier_semaphore()
-    neighbours = (
-        {"gx": x_right},
-        {"gx": x_left},
-        {"gy": y_right},
-        {"gy": y_left},
-        {"gz": other},
-    )
-    for neighbour in neighbours:
-        pl.semaphore_signal(barrier, inc=1, device_id=neighbour, device_id_type=MESH)
+    greeted = 0
+    for step_x in range(n_gx):
+        for step_z in range(2):
+            if step_x + step_z > 0:
+                friend = {"gx": lax.rem(gx + step_x, n_gx), "gz": lax.rem(gz + step_z, 2)}
+                pl.semaphore_signal(barrier, inc=1, device_id=friend, device_id_type=MESH)
+                greeted += 1
+    for step_y in range(1, n_gy):
+        friend = {"gy": lax.rem(gy + step_y, n_gy)}
+        pl.semaphore_signal(barrier, inc=1, device_id=friend, device_id_type=MESH)
+        greeted += 1
+
+    tile_rows = tiles * LANES
+    row_places = lax.broadcasted_iota(jnp.int32, (1, tile_rows), 1) + gy * tile_rows
+    waves[...] = waves_of(row_places.astype(jnp.float32))
+    for copy in column_copies:
+        copy.wait()
+    owners, lines, bands = codes[0:1, :], codes[1:2, :], codes[2:3, :]
+    column_count = meso.shape[1]
+    places = jnp.right_shift(owners, 1) * tile_rows + lines
+    column_waves = waves_of(places.astype(jnp.float32))
+    entries = meso.shape[0]
+    shifted = jnp.concatenate(
+        [meso[...], jnp.zeros((ENTRIES - entries, column_count), jnp.float32)], axis=0
+    )
+    for bit in range(4):
+        moved = pltpu.roll(shifted, ENTRIES - (1 << bit), 0)
+        chosen = jnp.bitwise_and(jnp.right_shift(bands, bit), 1) == 1
+        shifted = jnp.where(chosen, moved, shifted)
+    for side in range(2):
+        side_weight = jnp.where(jnp.bitwise_and(owners, 1) == side, col_weight[...], 0.0)
+        sum_send[side] = dot_rows(shifted * side_weight, column_waves)
+
+    pl.semaphore_wait(barrier, greeted)
+
+    def sum_copy(side, half_z):
+        return pltpu.make_async_remote_copy(
+            src_ref=sum_send.at[side, pl.ds(BAND_STEP * half_z, BAND_ROWS), :],
+            dst_ref=sum_recv.at[2 * gx + gz],
+            send_sem=ss_sem.at[side, half_z],
+            recv_sem=sr_sem.at[2 * gx + gz],
+            device_id={"gx": side * (n_gx - 1), "gz": half_z},
+            device_id_type=MESH,
+        )
+
+    def each_sum(act, act_here):
+        for side in range(2):
+            for half_z in range(2):
+                here = jnp.logical_and(gx == side * (n_gx - 1), gz == half_z)
+
+                @pl.when(jnp.logical_not(here))
+                def _():
+                    act(sum_copy(side, half_z))
+
+                if act_here is not None:
+
+                    @pl.when(here)
+                    def _():
+                        act_here(side, half_z)
+
+    def keep_sum(side, half_z):
+        start = BAND_STEP * half_z
+        sum_recv[2 * gx + gz] = sum_send[side, start : start + BAND_ROWS, :]
+
+    each_sum(lambda copy: copy.start(), keep_sum)
 
     zero_rows = pl.ds(pl.multiple_of(jnp.where(gz == 0, 0, ROWS + levels), ROWS), ROWS)
 
@@ -176,6 +287,90 @@
     lax.fori_loop(0, planes, blank, 0)
     y_send[...] = jnp.zeros_like(y_send)
     lane = lax.broadcasted_iota(jnp.int32, (ROWS, LANES), 1)
+
+    whole = state_a.at[pl.ds(tiles, planes), body_rows, :]
+    pltpu.make_async_copy(whole, whole, in_sem.at[0]).wait()
+
+    fringe = jnp.logical_or(west_end, east_end)
+    first = jnp.where(east_end, CX - FW, 0)
+    share = FW // n_gy
+
+    def part_copy(peer):
+        return pltpu.make_async_remote_copy(
+            src_ref=part.at[pl.ds(peer * share, share)],
+            dst_ref=part_recv.at[gy],
+            send_sem=ps_sem.at[peer],
+            recv_sem=pr_sem.at[gy],
+            device_id={"gy": peer},
+            device_id_type=MESH,
+        )
+
+    def part_arrival(peer):
+        return pltpu.make_async_remote_copy(
+            src_ref=part.at[pl.ds(peer * share, share)],
+            dst_ref=part_recv.at[peer],
+            send_sem=ps_sem.at[peer],
+            recv_sem=pr_sem.at[peer],
+            device_id={"gy": peer},
+            device_id_type=MESH,
+        )
+
+    def coef_copy(peer, owner):
+        return pltpu.make_async_remote_copy(
+            src_ref=coef.at[pl.ds(owner * share, share)],
+            dst_ref=coef.at[pl.ds(owner * share, share)],
+            send_sem=cs_sem.at[peer],
+            recv_sem=cr_sem.at[owner],
+            device_id={"gy": peer},
+            device_id_type=MESH,
+        )
+
+    peers = [lax.rem(gy + step_y, n_gy) for step_y in range(1, n_gy)]
+
+    @pl.when(fringe)
+    def _():
+        def strip_spectrum(index, carry):
+            base = (first + index + 1) * tiles
+            strip = jnp.concatenate(
+                [state_a[base + tile, body_rows, :] for tile in range(tiles)], axis=1
+            )
+            part[index] = dot_rows(strip, waves[...])
+            return carry
+
+        lax.fori_loop(0, FW, strip_spectrum, 0)
+
+        total = jnp.zeros((BAND_ROWS, 2 * KM), jnp.float32)
+        for slot in range(2 * n_gx):
+
+            @pl.when(slot != 2 * gx + gz)
+            def _():
+                pltpu.make_async_remote_copy(
+                    src_ref=sum_send.at[0, pl.ds(0, BAND_ROWS), :],
+                    dst_ref=sum_recv.at[slot],
+                    send_sem=ss_sem.at[0, 0],
+                    recv_sem=sr_sem.at[slot],
+                    device_id={"gz": other},
+                    device_id_type=MESH,
+                ).wait_recv()
+
+        for slot in range(2 * n_gx):
+            total = total + sum_recv[slot]
+        level = lax.broadcasted_iota(jnp.int32, (levels, BAND_ROWS), 0) + gz * levels
+        entry = lax.broadcasted_iota(jnp.int32, (levels, BAND_ROWS), 1) + gz * BAND_STEP
+        lower = jnp.right_shift(3 * level, 3)
+        fraction = jnp.bitwise_and(3 * level, 7).astype(jnp.float32) * 0.125
+        band = jnp.where(entry == lower, 1.0 - fraction, 0.0) + jnp.where(
+            entry == lower + 1, fraction, 0.0
+        )
+        target = jnp.dot(band, total, precision=highest, preferred_element_type=jnp.float32)
+
+        def subtract(index, carry):
+            part[index] = target - part[index]
+            return carry
+
+        lax.fori_loop(0, FW, subtract, 0)
+        for peer in peers:
+            part_copy(peer).start()
 
     courant_copy.wait()
 
@@ -194,18 +389,30 @@
 
     lax.fori_loop(0, planes, weigh, 0)
 
-    whole = state_a.at[pl.ds(tiles, planes), body_rows, :]
-    pltpu.make_async_copy(whole, whole, in_sem.at[0]).wait()
-    coef_copy.wait()
-    waves_copy.wait()
-
-    @pl.when(jnp.logical_or(west_end, east_end))
+    @pl.when(fringe)
     def _():
-        first = jnp.where(east_end, CX - FW, 0)
+        for peer in peers:
+            part_arrival(peer).wait_recv()
+        mode = lax.broadcasted_iota(jnp.int32, (levels, 2 * KM), 1)
+        scale = jnp.where(jnp.bitwise_and(mode, KM - 1) == 0, 1.0 / NY, 2.0 / NY)
+        for index in range(share):
+            plane = gy * share + index
+            total = part[plane]
+            for peer in peers:
+                total = total + part_recv[peer, index]
+            steps = jnp.where(east_end, plane + 1, FW - plane).astype(jnp.float32)
+            coef[plane] = (total * (scale * (steps * (1.0 / FW)))).astype(jnp.bfloat16)
+        for peer in peers:
+            coef_copy(peer, gy).start()
+        for peer in peers:
+            coef_copy(peer, peer).wait_recv()
 
         def nudge(index, carry):
             smooth = jnp.dot(
-                coef[index], waves[...], precision=highest, preferred_element_type=jnp.float32
+                coef[index].astype(jnp.float32),
+                waves[...],
+                precision=highest,
+                preferred_element_type=jnp.float32,
             )
             base = (first + index + 1) * tiles
             for tile in range(tiles):
@@ -272,8 +479,6 @@
             for tile in range(tiles):
                 x_send[step, side, tile] = state[base + tile, body_rows, :].astype(jnp.bfloat16)
             x_copy(step, side).start()
-
-    pl.semaphore_wait(barrier, len(neighbours))
 
     def plane_of(turn):
         plane = jnp.where(turn < 2 * half, turn + 1, jnp.where(turn == 2 * half, 0, CX - 1))
@@ -398,33 +603,53 @@
         return carry
 
     lax.fori_loop(0, NSTEP, settle, 0)
+    each_sum(lambda copy: copy.wait_send(), None)
+
+    @pl.when(fringe)
+    def _():
+        for peer in peers:
+            part_copy(peer).wait_send()
+            coef_copy(peer, gy).wait_send()
+
     pltpu.make_async_copy(whole, whole, out_sem).wait()
 
 
-def fast_sweep(theta, courants, coef, waves, n_gx, n_gy, tile_rows):
+def fast_sweep(theta, courants, meso, col_weight, codes, n_gx, n_gy, tile_rows):
     levels = theta.shape[0]
     tiles = tile_rows // LANES
     planes = CX * tiles
     slots = (CX + 2) * tiles
+    share = FW // n_gy
+    f32, bf16 = jnp.float32, jnp.bfloat16
+    field = pltpu.VMEM((slots, levels + 2 * ROWS, LANES), f32)
+    faces = pltpu.VMEM((NSTEP, 2, tiles, levels, LANES), bf16)
+    lines = pltpu.VMEM((NSTEP + 1, 4, 2, ROWS, LANES), f32)
     dma = pltpu.SemaphoreType.DMA
     anywhere = pl.BlockSpec(memory_space=pl.ANY)
     return pl.pallas_call(
         functools.partial(sweep_kernel, (n_gx, n_gy, levels, tiles)),
-        out_shape=jax.ShapeDtypeStruct(theta.shape, jnp.float32),
-        in_specs=[anywhere] * 4,
+        out_shape=jax.ShapeDtypeStruct(theta.shape, f32),
+        in_specs=[anywhere] * 5,
         out_specs=anywhere,
         scratch_shapes=[
-            pltpu.VMEM((slots, levels + 2 * ROWS, LANES), jnp.float32),
-            pltpu.VMEM((slots, levels + 2 * ROWS, LANES), jnp.float32),
-            pltpu.VMEM((7, planes, levels, LANES), jnp.float32),
-            pltpu.VMEM(courants.shape, jnp.bfloat16),
-            pltpu.VMEM(coef.shape, jnp.float32),
-            pltpu.VMEM(waves.shape, jnp.float32),
-            pltpu.VMEM((NSTEP, 2, tiles, levels, LANES), jnp.bfloat16),
-            pltpu.VMEM((NSTEP, 2, tiles, levels, LANES), jnp.bfloat16),
-            pltpu.VMEM((NSTEP + 1, 4, 2, ROWS, LANES), jnp.float32),
-            pltpu.VMEM((NSTEP, 4, 2, ROWS, LANES), jnp.float32),
-            dma((4,)),
+            field,
+            field,
+            pltpu.VMEM((7, planes, levels, LANES), f32),
+            pltpu.VMEM(courants.shape, bf16),
+            pltpu.VMEM(meso.shape, f32),
+            pltpu.VMEM(col_weight.shape, f32),
+            pltpu.VMEM(codes.shape, jnp.int32),
+            pltpu.VMEM((2 * KM, tile_rows), f32),
+            pltpu.VMEM((2, ENTRIES, 2 * KM), f32),
+            pltpu.VMEM((2 * n_gx, BAND_ROWS, 2 * KM), f32),
+            pltpu.VMEM((FW, levels, 2 * KM), f32),
+            pltpu.VMEM((n_gy, share, levels, 2 * KM), f32),
+            pltpu.VMEM((FW, levels, 2 * KM), bf16),
+            faces,
+            faces,
+            lines,
+            lines,
+            dma((5,)),
             dma,
             dma((NSTEP, 2)),
             dma((NSTEP, 2)),
@@ -432,12 +657,18 @@
             dma((NSTEP, 4, 2)),
             dma((NSTEP, 4)),
             dma((NSTEP, 4)),
+            dma((2, 2)),
+            dma((2 * n_gx,)),
+            dma((n_gy,)),
+            dma((n_gy,)),
+            dma((n_gy,)),
+            dma((n_gy,)),
         ],
         compiler_params=pltpu.CompilerParams(
             collective_id=0, has_side_effects=True, vmem_limit_bytes=58 * 1024 * 1024
         ),
         name="transport",
-    )(theta, courants, coef, waves)
+    )(theta, courants, meso, col_weight, codes)
 
 
 def body(theta_field, courants, meso_columns, col_weight, owner_ids, line_ids, band_start):
@@ -450,6 +681,20 @@
     east_end = column_index == n_gx - 1
     west_end = column_index == 0
 
+    fits = tile_rows % LANES == 0 and levels == 64 and FW % n_gy == 0
+    if fits and n_gz == 2 and n_gx > 2 and n_gy > 2:
+        result = fast_sweep(
+            theta_local,
+            courant_local,
+            meso_columns,
+            col_weight[None, :],
+            jnp.stack([owner_ids[:, 0], line_ids, band_start]),
+            n_gx,
+            n_gy,
+            tile_rows,
+        )
+        return result.reshape(1, 1, levels, CX * tile_rows)
+
     sums = target_spectrum(meso_columns, col_weight, owner_ids, line_ids, band_start, tile_rows)
     sums = lax.psum(sums, ("gx", "gy", "gz"))
     side_sums = jnp.where(east_end, sums[:, 2 * KM :], sums[:, : 2 * KM])
@@ -469,12 +714,6 @@
         east_end, (offsets + 1.0) / FW, jnp.where(west_end, (FW - offsets) / FW, 0.0)
     )
     coef = spectrum * mode_scale()[None, None, :] * relaxation[:, None, None]
-
-    if tile_rows % LANES == 0 and levels == 64 and n_gz == 2 and n_gx > 2 and n_gy > 2:
-        result = fast_sweep(
-            theta_local, courant_local, coef, own_waves.T, n_gx, n_gy, tile_rows
-        )
-        return result.reshape(1, 1, levels, CX * tile_rows)
 
     update = jnp.einsum(
         "xkm,ym->kxy", coef, own_waves, precision=highest, preferred_element_type=jnp.float32

time: 110 us -> 60.1 us (0.55)
  blocking collectives: 42.6 us -> 0 us
  Pallas kernels: 37.4 us -> 54.7 us
  between operations: 13.6 us -> 0.01 us
  other arithmetic: 8.58 us -> 1.34 us
  matrix products: 3.37 us -> 0 us
    psum x1 -> x0, blocking collectives: 42.6 us -> none  [body(): sums = lax.psum(sums, ('gx', 'gy', 'gz'))]
    pallas_call x1, Pallas kernels: 37.4 us -> 54.7 us  [fast_sweep(): pl.pallas_call(functools.partial(sweep_kernel, (n_gx, n_gy, levels, tiles...]
    dot_general x3 -> x0, matrix products: 3.37 us -> none  [the longest x1 2.08 us: body(): jnp.einsum('xky,ym->xkm', strip, own_waves, precision=highest, preferred_...]
    cos x2 -> x0, other arithmetic: 2.98 us -> none  [waves_at(): return jnp.concatenate([jnp.cos(angles), jnp.sin(angles)], axis=1)]
    select_n x5 -> x0, other arithmetic: 2.97 us -> none  [the longest x1 2.05 us: body(): strip = jnp.where(east_end, theta_local[:, -width:], theta_local[:, :width])]
    mul x1 -> x0, other arithmetic: 1.74 us -> none  [body(): coef = spectrum * mode_scale()[None, None, :] * relaxation[:, None, None]]
    another operation x0 -> x1, other arithmetic: none -> 1.34 us  [body(): jnp.stack([owner_ids[:, 0], line_ids, band_start])]
    unnamed x11 -> x1, local copies, waits for them, and re-layouts: 3.81 us -> 3.78 us
  transfers between devices with their start and end apart: 1 -> 0, of which waited for: 0 -> 0; matrix products, arithmetic and copies ran while one was open for 5% -> 0% of each run, Pallas kernels for 0% -> 0%
where the time goes in v2:
time: 60.1 us; the launch traced here: 59.9 us
  Pallas kernels  54.7 us (91%)
  local copies, waits for them, and re-layouts  3.78 us (6%)
  other arithmetic  1.34 us (2%)
    pallas_call x1, Pallas kernels, fast_sweep(): pl.pallas_call(functools.partial(sweep_kernel, (n_gx, n_gy, levels, tiles...  54.7 us
    unnamed x1, local copies, waits for them, and re-layouts  3.78 us
    another operation x1, other arithmetic, body(): jnp.stack([owner_ids[:, 0], line_ids, band_start])  1.34 us

profile of v2, /device:TPU:0, one launch (start us, length us, event | category | flops | bytes accessed | tf_op | source)
XLA Modules:
  0.0 59.9 jit_solution(4369273336691075749)
XLA Ops:
  0.0 1.3 %pad_add_fusion.codes_ref = s32[3,1024]{1,0:T(4,128)} fusion(s32[1,1024]{1,0:T(1,128)} %bitcast.11, s32[1,1024]{1,0:T(1,128)} %bitcast.12, s32[1,1024]{1,0:T(1,128)} %bitcast.13), kind=kLoop, calls=%fused_computation | loop fusion | flops 6144 | bytes 24576 | tf_op jit(solution)/shard_map/stack | solution.py:691
  1.3 54.7 %transport.1 = f32[64,12288]{1,0:T(8,128)} custom-call(f32[64,12288]{1,0:T(8,128)} %bitcast.9, bf16[3,64,12288]{2,1,0:T(8,128)(2,1)} %bitcast.8, f32[60,1024]{1,0:T(8,128)} %meso_ref.1, f32[1,1024]{1,0:T(1,128)} %bitcast.10, s32[3,1024]{1,0:T(4,128)} %pad_add_fusion.codes_ref), custom_call_target="tpu_custom_call" | custom-call | tf_op jit(solution)/shard_map/transport/pallas_call | solution.py:629
  56.1 3.8 %copy.9 = f32[1,1,64,12288]{3,2,1,0:T(8,128)} copy(f32[1,1,64,12288]{3,2,1,0:T(8,128)} %bitcast.7) | data formatting | bytes 6291456

commit v3 on v2

--- a/solution.py
+++ b/solution.py
@@ -126,14 +126,16 @@
     return jnp.concatenate([cos_values, sin_values], axis=0)
 
 
-def dot_rows(left, right):
-    return lax.dot_general(
-        left,
-        right,
-        (((1,), (1,)), ((), ())),
-        precision=highest,
-        preferred_element_type=jnp.float32,
-    )
+def in_two(values):
+    high = values.astype(jnp.bfloat16)
+    return high, (values - high.astype(jnp.float32)).astype(jnp.bfloat16)
+
+
+def dot_two(left, right, dims):
+    def one(a, b):
+        return lax.dot_general(a, b, (dims, ((), ())), preferred_element_type=jnp.float32)
+
+    return one(left[0], right[0]) + (one(left[1], right[0]) + one(left[0], right[1]))
 
 
 def sweep_kernel(
@@ -151,7 +153,9 @@
     meso,
     col_weight,
     codes,
-    waves,
+    waves_to,
+    waves_back,
+    strips,
     sum_send,
     sum_recv,
     part,
@@ -225,7 +229,11 @@
 
     tile_rows = tiles * LANES
     row_places = lax.broadcasted_iota(jnp.int32, (1, tile_rows), 1) + gy * tile_rows
-    waves[...] = waves_of(row_places.astype(jnp.float32))
+    row_waves = waves_of(row_places.astype(jnp.float32))
+    for piece, values in enumerate(in_two(row_waves)):
+        waves_back[piece * 2 * KM : (piece + 1) * 2 * KM, :] = values
+    for piece, values in enumerate(in_two(row_waves.T)):
+        waves_to[piece] = values
     for copy in column_copies:
         copy.wait()
     owners, lines, bands = codes[0:1, :], codes[1:2, :], codes[2:3, :]
@@ -240,9 +248,15 @@
         moved = pltpu.roll(shifted, ENTRIES - (1 << bit), 0)
         chosen = jnp.bitwise_and(jnp.right_shift(bands, bit), 1) == 1
         shifted = jnp.where(chosen, moved, shifted)
-    for side in range(2):
-        side_weight = jnp.where(jnp.bitwise_and(owners, 1) == side, col_weight[...], 0.0)
-        sum_send[side] = dot_rows(shifted * side_weight, column_waves)
+    sides = [
+        shifted * jnp.where(jnp.bitwise_and(owners, 1) == side, col_weight[...], 0.0)
+        for side in range(2)
+    ]
+    sums = dot_two(
+        in_two(jnp.concatenate(sides, axis=0)), in_two(column_waves), ((1,), (1,))
+    )
+    sum_send[0] = sums[:ENTRIES]
+    sum_send[1] = sums[ENTRIES:]
 
     pl.semaphore_wait(barrier, greeted)
 
@@ -291,6 +305,38 @@
     whole = state_a.at[pl.ds(tiles, planes), body_rows, :]
     pltpu.make_async_copy(whole, whole, in_sem.at[0]).wait()
 
+    part_rows = levels // 2
+
+    def x_copy(step, side, piece):
+        target = jnp.where(side == 0, x_right, x_left)
+        return pltpu.make_async_remote_copy(
+            src_ref=x_send.at[step, side, piece],
+            dst_ref=x_recv.at[step, side, piece],
+            send_sem=xs_sem.at[step, side, piece],
+            recv_sem=xr_sem.at[step, side, piece],
+            device_id={"gx": target},
+            device_id_type=MESH,
+        )
+
+    def send_face(state, step, side, piece):
+        base = ((1 - side) * (CX - 1) + 1) * tiles
+        rows = pl.ds(ROWS + piece * part_rows, part_rows)
+        for tile in range(tiles):
+            x_send[step, side, piece, tile] = state[base + tile, rows, :].astype(jnp.bfloat16)
+        x_copy(step, side, piece).start()
+
+    def send_faces(side):
+        for piece in range(2):
+            send_face(state_a, 0, side, piece)
+
+    @pl.when(jnp.logical_not(east_end))
+    def _():
+        send_faces(0)
+
+    @pl.when(jnp.logical_not(west_end))
+    def _():
+        send_faces(1)
+
     fringe = jnp.logical_or(west_end, east_end)
     first = jnp.where(east_end, CX - FW, 0)
     share = FW // n_gy
@@ -334,10 +380,16 @@
             strip = jnp.concatenate(
                 [state_a[base + tile, body_rows, :] for tile in range(tiles)], axis=1
             )
-            part[index] = dot_rows(strip, waves[...])
+            at = pl.ds(pl.multiple_of(index * levels, levels), levels)
+            for piece, values in enumerate(in_two(strip)):
+                strips[piece, at, :] = values
             return carry
 
         lax.fori_loop(0, FW, strip_spectrum, 0)
+        spectrum = dot_two(
+            (strips[0], strips[1]), (waves_to[0], waves_to[1]), ((1,), (0,))
+        )
+        part[...] = spectrum.reshape(part.shape)
 
         total = jnp.zeros((BAND_ROWS, 2 * KM), jnp.float32)
         for slot in range(2 * n_gx):
@@ -407,19 +459,29 @@
         for peer in peers:
             coef_copy(peer, peer).wait_recv()
 
-        def nudge(index, carry):
+        both = coef[...].reshape(FW * levels, 2 * KM)
+        both = jnp.concatenate([both, both], axis=1)
+        for start in range(0, tiles, 2):
+            stop = min(start + 2, tiles)
             smooth = jnp.dot(
-                coef[index].astype(jnp.float32),
-                waves[...],
-                precision=highest,
+                both,
+                waves_back[:, start * LANES : stop * LANES],
                 preferred_element_type=jnp.float32,
             )
-            base = (first + index + 1) * tiles
-            for tile in range(tiles):
-                state_a[base + tile, body_rows, :] += smooth[:, tile * LANES : (tile + 1) * LANES]
-            return carry
-
-        lax.fori_loop(0, FW, nudge, 0)
+            for index in range(FW):
+                own = slice(index * levels, (index + 1) * levels)
+                for tile in range(start, stop):
+                    at = (first + index + 1) * tiles + tile
+                    where = slice((tile - start) * LANES, (tile - start + 1) * LANES)
+                    state_a[at, body_rows, :] += smooth[own, where]
+
+    @pl.when(east_end)
+    def _():
+        send_faces(0)
+
+    @pl.when(west_end)
+    def _():
+        send_faces(1)
 
     source_rows = pl.ds(pl.multiple_of(jnp.where(gz == 0, levels, ROWS), ROWS), ROWS)
     target_rows = pl.ds(pl.multiple_of(jnp.where(gz == 0, 0, ROWS + levels), ROWS), ROWS)
@@ -446,22 +508,12 @@
             device_id_type=MESH,
         )
 
-    def x_copy(step, side):
-        return pltpu.make_async_remote_copy(
-            src_ref=x_send.at[step, side],
-            dst_ref=x_recv.at[step, side],
-            send_sem=xs_sem.at[step, side],
-            recv_sem=xr_sem.at[step, side],
-            device_id={"gx": x_right if side == 0 else x_left},
-            device_id_type=MESH,
-        )
-
     half = (CX - 2) // 2
     groups = ((1, half), (1 + half, half), (0, 1), (CX - 1, 1))
 
     def pack(step, group, plane, edges):
         right, left = y_send[step, group, 0], y_send[step, group, 1]
-        for chunk, (low, high) in enumerate(edges):
+        for chunk, low, high in edges:
             place = plane + chunk * CX
             here = lane == place
             right = jnp.where(here, pltpu.roll(high, lax.rem(place + 1, LANES), 1), right)
@@ -473,65 +525,60 @@
         z_copy(state, step, group).start()
         for side in range(2):
             y_copy(step, group, side).start()
-        if group >= 2:
-            side = 3 - group
-            base = (groups[group][0] + 1) * tiles
-            for tile in range(tiles):
-                x_send[step, side, tile] = state[base + tile, body_rows, :].astype(jnp.bfloat16)
-            x_copy(step, side).start()
-
-    def plane_of(turn):
-        plane = jnp.where(turn < 2 * half, turn + 1, jnp.where(turn == 2 * half, 0, CX - 1))
-        group = jnp.where(
-            turn < half, 0, jnp.where(turn < 2 * half, 1, jnp.where(turn == 2 * half, 2, 3))
-        )
-        return plane, group
-
-    def pack_start(turn, carry):
-        plane, group = plane_of(turn)
-        base = (plane + 1) * tiles
-        edges = []
-        for chunk in range(chunks):
-            rows = pl.ds(ROWS + chunk * ROWS, ROWS)
-            edges.append((state_a[base, rows, :], state_a[base + tiles - 1, rows, :]))
-        pack(0, group, plane, edges)
-        return carry
-
-    lax.fori_loop(0, CX, pack_start, 0)
-    for group in (2, 3, 0, 1):
+
+    def pack_planes(group):
+        first_plane, count = groups[group]
+
+        def pack_start(plane, carry):
+            base = (plane + 1) * tiles
+            edges = []
+            for chunk in range(chunks):
+                rows = pl.ds(ROWS + chunk * ROWS, ROWS)
+                edges.append((chunk, state_a[base, rows, :], state_a[base + tiles - 1, rows, :]))
+            pack(0, group, plane, edges)
+            return carry
+
+        lax.fori_loop(first_plane, first_plane + count, pack_start, 0)
         send(state_a, 0, group)
 
-    starts = (0, half, 2 * half, 2 * half + 1)
+    for group in range(4):
+        pack_planes(group)
 
     def advance(step, now, later, final):
-        def one(turn, carry):
-            plane, group = plane_of(turn)
-            for which in range(4):
-
-                @pl.when(turn == starts[which])
+        going_on = step < NSTEP - 1
+
+        def arrive(group):
+            z_copy(now, step, group).wait_recv()
+            for side in range(2):
+                y_copy(step, group, side).wait_recv()
+
+            @pl.when(step > 0)
+            def _():
+                z_copy(later, step - 1, group).wait_send()
+
+        def send_next(group):
+            @pl.when(going_on)
+            def _():
+                send(later, step + 1, group)
+
+        def put_out(plane):
+            if final:
+
+                @pl.when(step == NSTEP - 1)
                 def _():
-                    z_copy(now, step, which).wait_recv()
-                    for side in range(2):
-                        y_copy(step, which, side).wait_recv()
-
-                    @pl.when(step > 0)
-                    def _():
-                        z_copy(later, step - 1, which).wait_send()
-
-                    if which >= 2:
-                        side = which - 2
-                        x_copy(step, side).wait_recv()
-                        base = 0 if side == 0 else (CX + 1) * tiles
-                        for tile in range(tiles):
-                            now[base + tile, body_rows, :] = x_recv[step, side, tile].astype(
-                                jnp.float32
-                            )
-
+                    for tile in range(tiles):
+                        pltpu.make_async_copy(
+                            later.at[(plane + 1) * tiles + tile, body_rows, :],
+                            out_ref.at[:, tile_lanes(plane * tiles + tile)],
+                            out_sem,
+                        ).start()
+
+        def move(plane, group, some):
             base = (plane + 1) * tiles
             from_left = y_recv[step, group, 0]
             from_right = y_recv[step, group, 1]
             edges = []
-            for chunk in range(chunks):
+            for chunk in some:
                 row = ROWS + chunk * ROWS
                 rows = pl.ds(row, ROWS)
                 own = pl.ds(chunk * ROWS, ROWS)
@@ -560,30 +607,45 @@
                     )
                     later[at, rows, :] = total
                     results.append(total)
-                edges.append((results[0], results[-1]))
+                edges.append((chunk, results[0], results[-1]))
             pack(step + 1, group, plane, edges)
 
-            for which in range(4):
-                end = starts[which + 1] if which < 3 else CX
-
-                @pl.when(jnp.logical_and(turn == end - 1, step < NSTEP - 1))
+        for piece in range(2):
+            arrive(piece)
+            first_plane, count = groups[piece]
+
+            def inner(plane, carry):
+                move(plane, piece, range(chunks))
+                put_out(plane)
+                return carry
+
+            lax.fori_loop(first_plane, first_plane + count, inner, 0)
+            send_next(piece)
+            if piece == 0:
+                arrive(2)
+                arrive(3)
+            some = range(piece * chunks // 2, (piece + 1) * chunks // 2)
+            rows = pl.ds(ROWS + piece * part_rows, part_rows)
+
+            def edge(end, carry):
+                plane = end * (CX - 1)
+                x_copy(step, end, piece).wait_recv()
+                base = end * (CX + 1) * tiles
+                for tile in range(tiles):
+                    now[base + tile, rows, :] = x_recv[step, end, piece, tile].astype(jnp.float32)
+                move(plane, 2 + end, some)
+
+                @pl.when(going_on)
                 def _():
-                    send(later, step + 1, which)
-
-            if final:
-
-                @pl.when(step == NSTEP - 1)
-                def _():
-                    for tile in range(tiles):
-                        pltpu.make_async_copy(
-                            later.at[base + tile, body_rows, :],
-                            out_ref.at[:, tile_lanes(plane * tiles + tile)],
-                            out_sem,
-                        ).start()
-
-            return carry
-
-        lax.fori_loop(0, CX, one, 0)
+                    send_face(later, step + 1, 1 - end, piece)
+
+                if piece == 1:
+                    put_out(plane)
+                return carry
+
+            lax.fori_loop(0, 2, edge, 0)
+        send_next(2)
+        send_next(3)
 
     def two(pair, carry):
         advance(2 * pair, state_a, state_b, False)
@@ -597,7 +659,8 @@
 
     def settle(step, carry):
         for side in range(2):
-            x_copy(step, side).wait_send()
+            for piece in range(2):
+                x_copy(step, side, piece).wait_send()
             for group in range(4):
                 y_copy(step, group, side).wait_send()
         return carry
@@ -622,7 +685,7 @@
     share = FW // n_gy
     f32, bf16 = jnp.float32, jnp.bfloat16
     field = pltpu.VMEM((slots, levels + 2 * ROWS, LANES), f32)
-    faces = pltpu.VMEM((NSTEP, 2, tiles, levels, LANES), bf16)
+    faces = pltpu.VMEM((NSTEP, 2, 2, tiles, levels // 2, LANES), bf16)
     lines = pltpu.VMEM((NSTEP + 1, 4, 2, ROWS, LANES), f32)
     dma = pltpu.SemaphoreType.DMA
     anywhere = pl.BlockSpec(memory_space=pl.ANY)
@@ -639,7 +702,9 @@
             pltpu.VMEM(meso.shape, f32),
             pltpu.VMEM(col_weight.shape, f32),
             pltpu.VMEM(codes.shape, jnp.int32),
-            pltpu.VMEM((2 * KM, tile_rows), f32),
+            pltpu.VMEM((2, tile_rows, 2 * KM), bf16),
+            pltpu.VMEM((4 * KM, tile_rows), bf16),
+            pltpu.VMEM((2, FW * levels, tile_rows), bf16),
             pltpu.VMEM((2, ENTRIES, 2 * KM), f32),
             pltpu.VMEM((2 * n_gx, BAND_ROWS, 2 * KM), f32),
             pltpu.VMEM((FW, levels, 2 * KM), f32),
@@ -651,8 +716,8 @@
             lines,
             dma((5,)),
             dma,
-            dma((NSTEP, 2)),
-            dma((NSTEP, 2)),
+            dma((NSTEP, 2, 2)),
+            dma((NSTEP, 2, 2)),
             dma((NSTEP, 4, 2)),
             dma((NSTEP, 4, 2)),
             dma((NSTEP, 4)),

time: 60.1 us -> 56.5 us (0.940)
  Pallas kernels: 54.7 us -> 51.2 us
    pallas_call x1, Pallas kernels: 54.7 us -> 51.2 us  [fast_sweep(): pl.pallas_call(functools.partial(sweep_kernel, (n_gx, n_gy, levels, tiles...]
where the time goes in v3:
time: 56.5 us; the launch traced here: 56.3 us
  Pallas kernels  51.2 us (91%)
  local copies, waits for them, and re-layouts  3.78 us (7%)
  other arithmetic  1.34 us (2%)
    pallas_call x1, Pallas kernels, fast_sweep(): pl.pallas_call(functools.partial(sweep_kernel, (n_gx, n_gy, levels, tiles...  51.2 us
    unnamed x1, local copies, waits for them, and re-layouts  3.78 us
    another operation x1, other arithmetic, body(): jnp.stack([owner_ids[:, 0], line_ids, band_start])  1.34 us

profile of v3, /device:TPU:0, one launch (start us, length us, event | category | flops | bytes accessed | tf_op | source)
XLA Modules:
  0.0 56.3 jit_solution(13756942635668542780)
XLA Ops:
  0.0 1.3 %pad_add_fusion.codes_ref = s32[3,1024]{1,0:T(4,128)} fusion(s32[1,1024]{1,0:T(1,128)} %bitcast.11, s32[1,1024]{1,0:T(1,128)} %bitcast.12, s32[1,1024]{1,0:T(1,128)} %bitcast.13), kind=kLoop, calls=%fused_computation | loop fusion | flops 6144 | bytes 24576 | tf_op jit(solution)/shard_map/stack | solution.py:756
  1.3 51.2 %transport.1 = f32[64,12288]{1,0:T(8,128)} custom-call(f32[64,12288]{1,0:T(8,128)} %bitcast.9, bf16[3,64,12288]{2,1,0:T(8,128)(2,1)} %bitcast.8, f32[60,1024]{1,0:T(8,128)} %meso_ref.1, f32[1,1024]{1,0:T(1,128)} %bitcast.10, s32[3,1024]{1,0:T(4,128)} %pad_add_fusion.codes_ref), custom_call_target="tpu_custom_call" | custom-call | tf_op jit(solution)/shard_map/transport/pallas_call | solution.py:692
  52.5 3.8 %copy.9 = f32[1,1,64,12288]{3,2,1,0:T(8,128)} copy(f32[1,1,64,12288]{3,2,1,0:T(8,128)} %bitcast.7) | data formatting | bytes 6291456

commit v4 on v3

--- a/solution.py
+++ b/solution.py
@@ -144,7 +144,9 @@
     courant_ref,
     meso_ref,
     col_weight_ref,
-    codes_ref,
+    owner_ref,
+    line_ref,
+    band_ref,
     out_ref,
     state_a,
     state_b,
@@ -152,7 +154,9 @@
     courant,
     meso,
     col_weight,
-    codes,
+    owner_ids,
+    line_ids,
+    band_ids,
     waves_to,
     waves_back,
     strips,
@@ -166,7 +170,6 @@
     y_send,
     y_recv,
     in_sem,
-    out_sem,
     xs_sem,
     xr_sem,
     ys_sem,
@@ -198,7 +201,9 @@
     column_copies = [
         pltpu.make_async_copy(meso_ref, meso, in_sem.at[2]),
         pltpu.make_async_copy(col_weight_ref, col_weight, in_sem.at[3]),
-        pltpu.make_async_copy(codes_ref, codes, in_sem.at[4]),
+        pltpu.make_async_copy(owner_ref, owner_ids, in_sem.at[4]),
+        pltpu.make_async_copy(line_ref, line_ids, in_sem.at[5]),
+        pltpu.make_async_copy(band_ref, band_ids, in_sem.at[6]),
     ]
 
     def fetch(tile, carry):
@@ -208,11 +213,6 @@
             in_sem.at[0],
         ).start()
         return carry
-
-    for copy in column_copies:
-        copy.start()
-    lax.fori_loop(0, planes, fetch, 0)
-    courant_copy.start()
 
     barrier = pltpu.get_barrier_semaphore()
     greeted = 0
@@ -222,21 +222,22 @@
                 friend = {"gx": lax.rem(gx + step_x, n_gx), "gz": lax.rem(gz + step_z, 2)}
                 pl.semaphore_signal(barrier, inc=1, device_id=friend, device_id_type=MESH)
                 greeted += 1
+    partner = gx + 1 - 2 * lax.rem(gx, 2)
     for step_y in range(1, n_gy):
-        friend = {"gy": lax.rem(gy + step_y, n_gy)}
-        pl.semaphore_signal(barrier, inc=1, device_id=friend, device_id_type=MESH)
-        greeted += 1
+        for friend_x in (gx, partner):
+            friend = {"gx": friend_x, "gy": lax.rem(gy + step_y, n_gy)}
+            pl.semaphore_signal(barrier, inc=1, device_id=friend, device_id_type=MESH)
+            greeted += 1
+
+    for copy in column_copies:
+        copy.start()
+    lax.fori_loop(0, planes, fetch, 0)
+    courant_copy.start()
 
     tile_rows = tiles * LANES
-    row_places = lax.broadcasted_iota(jnp.int32, (1, tile_rows), 1) + gy * tile_rows
-    row_waves = waves_of(row_places.astype(jnp.float32))
-    for piece, values in enumerate(in_two(row_waves)):
-        waves_back[piece * 2 * KM : (piece + 1) * 2 * KM, :] = values
-    for piece, values in enumerate(in_two(row_waves.T)):
-        waves_to[piece] = values
     for copy in column_copies:
         copy.wait()
-    owners, lines, bands = codes[0:1, :], codes[1:2, :], codes[2:3, :]
+    owners, lines, bands = owner_ids[...], line_ids[...], band_ids[...]
     column_count = meso.shape[1]
     places = jnp.right_shift(owners, 1) * tile_rows + lines
     column_waves = waves_of(places.astype(jnp.float32))
@@ -291,6 +292,13 @@
 
     each_sum(lambda copy: copy.start(), keep_sum)
 
+    row_places = lax.broadcasted_iota(jnp.int32, (1, tile_rows), 1) + gy * tile_rows
+    row_waves = waves_of(row_places.astype(jnp.float32))
+    for piece, values in enumerate(in_two(row_waves)):
+        waves_back[piece * 2 * KM : (piece + 1) * 2 * KM, :] = values
+    for piece, values in enumerate(in_two(row_waves.T)):
+        waves_to[piece] = values
+
     zero_rows = pl.ds(pl.multiple_of(jnp.where(gz == 0, 0, ROWS + levels), ROWS), ROWS)
 
     def blank(tile, carry):
@@ -339,37 +347,56 @@
 
     fringe = jnp.logical_or(west_end, east_end)
     first = jnp.where(east_end, CX - FW, 0)
-    share = FW // n_gy
-
-    def part_copy(peer):
+    end_x = jnp.where(fringe, gx, partner)
+    helper_x = jnp.where(fringe, partner, gx)
+    my_plane = jnp.where(fringe, gy, n_gy + gy)
+
+    def part_copy(owner, peer):
+        plane = peer + owner * n_gy
         return pltpu.make_async_remote_copy(
-            src_ref=part.at[pl.ds(peer * share, share)],
+            src_ref=part.at[plane],
             dst_ref=part_recv.at[gy],
-            send_sem=ps_sem.at[peer],
+            send_sem=ps_sem.at[plane],
             recv_sem=pr_sem.at[gy],
-            device_id={"gy": peer},
+            device_id={"gx": helper_x if owner else end_x, "gy": peer},
             device_id_type=MESH,
         )
 
-    def part_arrival(peer):
+    def part_arrival(source):
         return pltpu.make_async_remote_copy(
-            src_ref=part.at[pl.ds(peer * share, share)],
-            dst_ref=part_recv.at[peer],
-            send_sem=ps_sem.at[peer],
-            recv_sem=pr_sem.at[peer],
-            device_id={"gy": peer},
+            src_ref=part.at[0],
+            dst_ref=part_recv.at[source],
+            send_sem=ps_sem.at[0],
+            recv_sem=pr_sem.at[source],
+            device_id={"gx": partner},
             device_id_type=MESH,
         )
 
-    def coef_copy(peer, owner):
+    def coef_copy(peer):
         return pltpu.make_async_remote_copy(
-            src_ref=coef.at[pl.ds(owner * share, share)],
-            dst_ref=coef.at[pl.ds(owner * share, share)],
+            src_ref=coef.at[my_plane],
+            dst_ref=coef.at[my_plane],
             send_sem=cs_sem.at[peer],
-            recv_sem=cr_sem.at[owner],
-            device_id={"gy": peer},
+            recv_sem=cr_sem.at[my_plane],
+            device_id={"gx": end_x, "gy": peer},
             device_id_type=MESH,
         )
+
+    def coef_arrival(plane):
+        return pltpu.make_async_remote_copy(
+            src_ref=coef.at[plane],
+            dst_ref=coef.at[plane],
+            send_sem=cs_sem.at[0],
+            recv_sem=cr_sem.at[plane],
+            device_id={"gx": partner},
+            device_id_type=MESH,
+        )
+
+    def scaled(total):
+        mode = lax.broadcasted_iota(jnp.int32, (levels, 2 * KM), 1)
+        scale = jnp.where(jnp.bitwise_and(mode, KM - 1) == 0, 1.0 / NY, 2.0 / NY)
+        steps = jnp.where(end_x == 0, FW - my_plane, my_plane + 1).astype(jnp.float32)
+        coef[my_plane] = (total * (scale * (steps * (1.0 / FW)))).astype(jnp.bfloat16)
 
     peers = [lax.rem(gy + step_y, n_gy) for step_y in range(1, n_gy)]
 
@@ -422,7 +449,9 @@
 
         lax.fori_loop(0, FW, subtract, 0)
         for peer in peers:
-            part_copy(peer).start()
+            part_copy(0, peer).start()
+            part_copy(1, peer).start()
+        part_copy(1, gy).start()
 
     courant_copy.wait()
 
@@ -445,19 +474,16 @@
     def _():
         for peer in peers:
             part_arrival(peer).wait_recv()
-        mode = lax.broadcasted_iota(jnp.int32, (levels, 2 * KM), 1)
-        scale = jnp.where(jnp.bitwise_and(mode, KM - 1) == 0, 1.0 / NY, 2.0 / NY)
-        for index in range(share):
-            plane = gy * share + index
-            total = part[plane]
-            for peer in peers:
-                total = total + part_recv[peer, index]
-            steps = jnp.where(east_end, plane + 1, FW - plane).astype(jnp.float32)
-            coef[plane] = (total * (scale * (steps * (1.0 / FW)))).astype(jnp.bfloat16)
+        total = part[gy]
         for peer in peers:
-            coef_copy(peer, gy).start()
+            total = total + part_recv[peer]
+        scaled(total)
         for peer in peers:
-            coef_copy(peer, peer).wait_recv()
+            coef_copy(peer).start()
+        for peer in peers:
+            coef_arrival(peer).wait_recv()
+        for peer in range(n_gy):
+            coef_arrival(n_gy + peer).wait_recv()
 
         both = coef[...].reshape(FW * levels, 2 * KM)
         both = jnp.concatenate([both, both], axis=1)
@@ -475,6 +501,17 @@
                     where = slice((tile - start) * LANES, (tile - start + 1) * LANES)
                     state_a[at, body_rows, :] += smooth[own, where]
 
+    @pl.when(jnp.logical_not(fringe))
+    def _():
+        for peer in range(n_gy):
+            part_arrival(peer).wait_recv()
+        total = part_recv[0]
+        for peer in range(1, n_gy):
+            total = total + part_recv[peer]
+        scaled(total)
+        for peer in range(n_gy):
+            coef_copy(peer).start()
+
     @pl.when(east_end)
     def _():
         send_faces(0)
@@ -560,18 +597,6 @@
             @pl.when(going_on)
             def _():
                 send(later, step + 1, group)
-
-        def put_out(plane):
-            if final:
-
-                @pl.when(step == NSTEP - 1)
-                def _():
-                    for tile in range(tiles):
-                        pltpu.make_async_copy(
-                            later.at[(plane + 1) * tiles + tile, body_rows, :],
-                            out_ref.at[:, tile_lanes(plane * tiles + tile)],
-                            out_sem,
-                        ).start()
 
         def move(plane, group, some):
             base = (plane + 1) * tiles
@@ -606,6 +631,8 @@
                         (terms[5] + terms[6]) + terms[0]
                     )
                     later[at, rows, :] = total
+                    if final:
+                        out_ref[own, tile_lanes(mine)] = total
                     results.append(total)
                 edges.append((chunk, results[0], results[-1]))
             pack(step + 1, group, plane, edges)
@@ -616,7 +643,6 @@
 
             def inner(plane, carry):
                 move(plane, piece, range(chunks))
-                put_out(plane)
                 return carry
 
             lax.fori_loop(first_plane, first_plane + count, inner, 0)
@@ -639,8 +665,6 @@
                 def _():
                     send_face(later, step + 1, 1 - end, piece)
 
-                if piece == 1:
-                    put_out(plane)
                 return carry
 
             lax.fori_loop(0, 2, edge, 0)
@@ -671,29 +695,33 @@
     @pl.when(fringe)
     def _():
         for peer in peers:
-            part_copy(peer).wait_send()
-            coef_copy(peer, gy).wait_send()
-
-    pltpu.make_async_copy(whole, whole, out_sem).wait()
-
-
-def fast_sweep(theta, courants, meso, col_weight, codes, n_gx, n_gy, tile_rows):
+            part_copy(0, peer).wait_send()
+            part_copy(1, peer).wait_send()
+            coef_copy(peer).wait_send()
+        part_copy(1, gy).wait_send()
+
+    @pl.when(jnp.logical_not(fringe))
+    def _():
+        for peer in range(n_gy):
+            coef_copy(peer).wait_send()
+
+
+def fast_sweep(theta, courants, meso, col_weight, owner, line, band, n_gx, n_gy, tile_rows):
     levels = theta.shape[0]
     tiles = tile_rows // LANES
     planes = CX * tiles
     slots = (CX + 2) * tiles
-    share = FW // n_gy
     f32, bf16 = jnp.float32, jnp.bfloat16
     field = pltpu.VMEM((slots, levels + 2 * ROWS, LANES), f32)
     faces = pltpu.VMEM((NSTEP, 2, 2, tiles, levels // 2, LANES), bf16)
     lines = pltpu.VMEM((NSTEP + 1, 4, 2, ROWS, LANES), f32)
     dma = pltpu.SemaphoreType.DMA
-    anywhere = pl.BlockSpec(memory_space=pl.ANY)
+    main_memory = pl.BlockSpec(memory_space=pltpu.HBM)
     return pl.pallas_call(
         functools.partial(sweep_kernel, (n_gx, n_gy, levels, tiles)),
-        out_shape=jax.ShapeDtypeStruct(theta.shape, f32),
-        in_specs=[anywhere] * 5,
-        out_specs=anywhere,
+        out_shape=pltpu.VMEM(theta.shape, f32),
+        in_specs=[main_memory] * 7,
+        out_specs=pl.BlockSpec(memory_space=pltpu.VMEM),
         scratch_shapes=[
             field,
             field,
@@ -701,21 +729,22 @@
             pltpu.VMEM(courants.shape, bf16),
             pltpu.VMEM(meso.shape, f32),
             pltpu.VMEM(col_weight.shape, f32),
-            pltpu.VMEM(codes.shape, jnp.int32),
+            pltpu.VMEM(owner.shape, jnp.int32),
+            pltpu.VMEM(line.shape, jnp.int32),
+            pltpu.VMEM(band.shape, jnp.int32),
             pltpu.VMEM((2, tile_rows, 2 * KM), bf16),
             pltpu.VMEM((4 * KM, tile_rows), bf16),
             pltpu.VMEM((2, FW * levels, tile_rows), bf16),
             pltpu.VMEM((2, ENTRIES, 2 * KM), f32),
             pltpu.VMEM((2 * n_gx, BAND_ROWS, 2 * KM), f32),
             pltpu.VMEM((FW, levels, 2 * KM), f32),
-            pltpu.VMEM((n_gy, share, levels, 2 * KM), f32),
+            pltpu.VMEM((n_gy, levels, 2 * KM), f32),
             pltpu.VMEM((FW, levels, 2 * KM), bf16),
             faces,
             faces,
             lines,
             lines,
-            dma((5,)),
-            dma,
+            dma((7,)),
             dma((NSTEP, 2, 2)),
             dma((NSTEP, 2, 2)),
             dma((NSTEP, 4, 2)),
@@ -724,16 +753,16 @@
             dma((NSTEP, 4)),
             dma((2, 2)),
             dma((2 * n_gx,)),
+            dma((FW,)),
             dma((n_gy,)),
             dma((n_gy,)),
-            dma((n_gy,)),
-            dma((n_gy,)),
+            dma((FW,)),
         ],
         compiler_params=pltpu.CompilerParams(
-            collective_id=0, has_side_effects=True, vmem_limit_bytes=58 * 1024 * 1024
+            collective_id=0, has_side_effects=True, vmem_limit_bytes=48 * 1024 * 1024
         ),
         name="transport",
-    )(theta, courants, meso, col_weight, codes)
+    )(theta, courants, meso, col_weight, owner, line, band)
 
 
 def body(theta_field, courants, meso_columns, col_weight, owner_ids, line_ids, band_start):
@@ -746,14 +775,16 @@
     east_end = column_index == n_gx - 1
     west_end = column_index == 0
 
-    fits = tile_rows % LANES == 0 and levels == 64 and FW % n_gy == 0
-    if fits and n_gz == 2 and n_gx > 2 and n_gy > 2:
+    fits = tile_rows % LANES == 0 and levels == 64 and FW == 2 * n_gy
+    if fits and n_gz == 2 and n_gx == 4 and n_gy > 2:
         result = fast_sweep(
             theta_local,
             courant_local,
             meso_columns,
             col_weight[None, :],
-            jnp.stack([owner_ids[:, 0], line_ids, band_start]),
+            owner_ids.reshape(1, -1),
+            line_ids[None, :],
+            band_start[None, :],
             n_gx,
             n_gy,
             tile_rows,

time: 56.5 us -> 56.5 us (level)
  local copies, waits for them, and re-layouts: 3.78 us -> 5.36 us
  other arithmetic: 1.34 us -> 0 us
    unnamed x1 -> x11, local copies, waits for them, and re-layouts: 3.78 us -> 5.36 us
    another operation x1 -> x0, other arithmetic: 1.34 us -> none  [body(): jnp.stack([owner_ids[:, 0], line_ids, band_start])]
where the time goes in v4:
time: 56.5 us; the launch traced here: 56.2 us
  Pallas kernels  50.8 us (90%)
  local copies, waits for them, and re-layouts  5.36 us (9%)
    pallas_call x1, Pallas kernels, fast_sweep(): pl.pallas_call(functools.partial(sweep_kernel, (n_gx, n_gy, levels, tiles...  50.8 us
    unnamed x11, local copies, waits for them, and re-layouts  5.36 us

profile of v4, /device:TPU:0, one launch (start us, length us, event | category | flops | bytes accessed | tf_op | source)
XLA Modules:
  0.0 56.2 jit_solution(8928229051335072440)
XLA Ops:
  0.0 0.0 copy-start
  0.0 0.9 %copy-done = f32[60,1024]{1,0:T(8,128)S(1)} copy-done((f32[60,1024]{1,0:T(8,128)S(1)}, f32[60,1024]{1,0:T(8,128)}, u32[]{:S(2)}) %copy-start) | copy-done | bytes 245784
  1.0 0.0 copy-start.1
  1.0 0.7 %copy-done.1 = f32[1024]{0:T(1024)S(1)} copy-done((f32[1024]{0:T(1024)S(1)}, f32[1024]{0:T(1024)}, u32[]{:S(2)}) %copy-start.1) | copy-done | bytes 4120
  1.6 0.0 copy-start.2
  1.6 0.7 %copy-done.2 = s32[1024,1]{0,1:T(1,128)S(1)} copy-done((s32[1024,1]{0,1:T(1,128)S(1)}, s32[1024,1]{0,1:T(1,128)}, u32[]{:S(2)}) %copy-start.2) | copy-done | bytes 4120
  2.3 0.0 copy-start.3
  2.3 0.7 %copy-done.3 = s32[1024]{0:T(1024)S(1)} copy-done((s32[1024]{0:T(1024)S(1)}, s32[1024]{0:T(1024)}, u32[]{:S(2)}) %copy-start.3) | copy-done | bytes 4120
  3.0 0.0 copy-start.4
  3.0 0.7 %copy-done.4 = s32[1024]{0:T(1024)S(1)} copy-done((s32[1024]{0:T(1024)S(1)}, s32[1024]{0:T(1024)}, u32[]{:S(2)}) %copy-start.4) | copy-done | bytes 4120
  3.7 50.8 %transport.1 = f32[64,12288]{1,0:T(8,128)S(1)} custom-call(f32[64,12288]{1,0:T(8,128)} %bitcast.13, bf16[3,64,12288]{2,1,0:T(8,128)(2,1)} %bitcast.12, f32[60,1024]{1,0:T(8,128)S(1)} %copy-done, f32[1,1024]{1,0:T(1,128)S(1)} %bitcast.8, s32[1,1024]{1,0:T(1,128)S(1)} %bitcast.9, s32[1,1024]{1,0:T(1,128)S(1)} %bitcast.10, s32[1,1024]{1,0:T(1,128)S(1)} %bitcast.11), custom_call_target="tpu_custom_call" | custom-call | tf_op jit(solution)/shard_map/transport/pallas_call | solution.py:720
  54.5 1.7 %copy.9 = f32[1,1,64,12288]{3,2,1,0:T(8,128)} copy(f32[1,1,64,12288]{3,2,1,0:T(8,128)S(1)} %bitcast.7) | data formatting | bytes 6291456
Async XLA Ops:
  0.0 0.9 %copy-start = (f32[60,1024]{1,0:T(8,128)S(1)}, f32[60,1024]{1,0:T(8,128)}, u32[]{:S(2)}) copy-start(f32[60,1024]{1,0:T(8,128)} %meso_ref.1) | copy-start | bytes 737284
  1.0 0.7 %copy-start.1 = (f32[1024]{0:T(1024)S(1)}, f32[1024]{0:T(1024)}, u32[]{:S(2)}) copy-start(f32[1024]{0:T(1024)} %param.10) | copy-start | bytes 12292
  1.6 0.7 %copy-start.2 = (s32[1024,1]{0,1:T(1,128)S(1)}, s32[1024,1]{0,1:T(1,128)}, u32[]{:S(2)}) copy-start(s32[1024,1]{0,1:T(1,128)} %param.11) | copy-start | bytes 12292
  2.3 0.7 %copy-start.3 = (s32[1024]{0:T(1024)S(1)}, s32[1024]{0:T(1024)}, u32[]{:S(2)}) copy-start(s32[1024]{0:T(1024)} %param.12) | copy-start | bytes 12292
  3.0 0.7 %copy-start.4 = (s32[1024]{0:T(1024)S(1)}, s32[1024]{0:T(1024)}, u32[]{:S(2)}) copy-start(s32[1024]{0:T(1024)} %param.13) | copy-start | bytes 12292

commit v5 on v4

--- a/solution.py
+++ b/solution.py
@@ -759,7 +759,7 @@
             dma((FW,)),
         ],
         compiler_params=pltpu.CompilerParams(
-            collective_id=0, has_side_effects=True, vmem_limit_bytes=48 * 1024 * 1024
+            collective_id=0, has_side_effects=True, vmem_limit_bytes=58 * 1024 * 1024
         ),
         name="transport",
     )(theta, courants, meso, col_weight, owner, line, band)

time: 56.5 us -> 53 us (0.938)
  local copies, waits for them, and re-layouts: 5.36 us -> 1.67 us
    unnamed x11 -> x1, local copies, waits for them, and re-layouts: 5.36 us -> 1.67 us
where the time goes in v5:
time: 53 us; the launch traced here: 52.9 us
  Pallas kernels  51.2 us (97%)
  local copies, waits for them, and re-layouts  1.67 us (3%)
    pallas_call x1, Pallas kernels, fast_sweep(): pl.pallas_call(functools.partial(sweep_kernel, (n_gx, n_gy, levels, tiles...  51.2 us
    unnamed x1, local copies, waits for them, and re-layouts  1.67 us

profile of v5, /device:TPU:0, one launch (start us, length us, event | category | flops | bytes accessed | tf_op | source)
XLA Modules:
  0.0 52.9 jit_solution(12189902503691137104)
XLA Ops:
  0.0 51.2 %transport.1 = f32[64,12288]{1,0:T(8,128)S(1)} custom-call(f32[64,12288]{1,0:T(8,128)} %bitcast.9, bf16[3,64,12288]{2,1,0:T(8,128)(2,1)} %bitcast.8, f32[60,1024]{1,0:T(8,128)} %meso_ref.1, f32[1,1024]{1,0:T(1,128)} %bitcast.10, s32[1,1024]{1,0:T(1,128)} %bitcast.11, s32[1,1024]{1,0:T(1,128)} %bitcast.12, s32[1,1024]{1,0:T(1,128)} %bitcast.13), custom_call_target="tpu_custom_call" | custom-call | tf_op jit(solution)/shard_map/transport/pallas_call | solution.py:720
  51.2 1.7 %copy.9 = f32[1,1,64,12288]{3,2,1,0:T(8,128)} copy(f32[1,1,64,12288]{3,2,1,0:T(8,128)S(1)} %bitcast.7) | data formatting | bytes 6291456
